TPU v7x, 1024 devices: a whole 4x8x16 slice. The times are simulated.
1024 devices in a mesh: blk: 256 (over y, z_lo, x), group: 4 (over z_hi, core).
Axes of the slice: x: 4, y: 8, z: 16 (z_hi: 2, z_lo: 8; z = z_hi * 8 + z_lo), core: 2. Of those that a mesh axis runs over, the one named last changes fastest.
Arguments:
- image: bfloat16 [131072, 1152], P(('blk', 'group')), may hold values from -0.1796875 to 0.1796875
- text: bfloat16 [131072, 1152], P(('blk', 'group')), may hold values from -0.1796875 to 0.1796875
- positives: int32 [131072], P(('blk', 'group')), may hold values from 0 to 127, as said below
- logit_scale: float32 [1], replicated, may hold values from 4 to 16
- logit_bias: float32 [1], replicated, may hold values from -4 to -1
Outputs:
- image_grad: float32 [131072, 1152], P(('blk', 'group'))
- text_grad: float32 [131072, 1152], P(('blk', 'group'))
Inputs may be any that keep to these rules, and one draw needn't show every extreme that they name: `positives`: each aligned block of 128 entries is a permutation of 0 to 127.
All inputs are finite; a program needn't handle non-finite values.
Results may differ from a plain program's by a relative error of at most 0.004.
Values may be sent and summed in bfloat16 or wider, within the bound.
No kernel may reach another device: no remote copies, remote signals or barrier semaphores. Data moves between devices by JAX's collectives and lax.ppermute only.
A program may use at most 32 MiB of HBM per device.

v0:
```python
import jax
import jax.numpy as jnp
from jax import lax
from jax.sharding import PartitionSpec as P

ROUNDS = 2


norm_eps = 1e-06


def shifted(value, axis, steps):
    count = lax.axis_size(axis)
    pairs = [(source, (source + steps) % count) for source in range(count)]
    return lax.ppermute(value, axis, pairs)


def unit_rows(values):
    wide = values.astype(jnp.float32)
    inverse = lax.rsqrt(jnp.sum(wide * wide, axis=-1, keepdims=True) + norm_eps)
    return (wide, inverse, (wide * inverse).astype(jnp.bfloat16))


def unit_backward(wide, inverse, upstream):
    inner = jnp.sum(wide * upstream, axis=-1, keepdims=True)
    return inverse * (upstream - inverse * inverse * wide * inner)


def local(image, text, positives, logit_scale, logit_bias):
    image_wide, image_inv, image_unit = unit_rows(image)
    text_wide, text_inv, text_unit = unit_rows(text)
    row_count = image.shape[0]
    width = image.shape[1]
    groups = lax.axis_size("group")
    logit_mult = logit_scale[0]
    logit_add = logit_bias[0]
    group_index = lax.axis_index("group")
    columns = lax.broadcasted_iota(jnp.int32, (row_count, groups * row_count), 1)
    target = (columns == (group_index * row_count + positives)[:, None]).astype(jnp.float32)
    image_acc = jnp.zeros((row_count, width), jnp.float32)
    returned = jnp.zeros((row_count, width), jnp.float32)
    met_text = lax.all_gather(text_unit, "group", axis=0, tiled=True)
    for turn_index in range(ROUNDS):
        if turn_index > 0:
            met_text = shifted(met_text, "blk", 1)
        logits = (
            logit_mult
            * lax.dot_general(
                image_unit, met_text, (((1,), (1,)), ((), ())), preferred_element_type=jnp.float32
            )
            + logit_add
        )
        weights = jax.nn.sigmoid(logits)
        if turn_index == 0:
            weights = weights - target
        coeff = weights.astype(jnp.bfloat16)
        image_acc = image_acc + logit_mult * jnp.dot(
            coeff, met_text, preferred_element_type=jnp.float32
        )
        text_term = logit_mult * lax.dot_general(
            coeff, image_unit, (((0,), (0,)), ((), ())), preferred_element_type=jnp.float32
        )
        own_sum = lax.psum_scatter(text_term, "group", scatter_dimension=0, tiled=True)
        if turn_index > 0:
            own_sum = shifted(own_sum, "blk", -turn_index)
        returned = returned + own_sum
    image_grad = unit_backward(image_wide, image_inv, image_acc)
    text_grad = unit_backward(text_wide, text_inv, returned)
    return (image_grad, text_grad)


def solution(mesh):
    in_specs = (P(("blk", "group"), None), P(("blk", "group"), None), P(("blk", "group")), P(), P())
    out_specs = (P(("blk", "group"), None), P(("blk", "group"), None))
    return jax.shard_map(local, mesh=mesh, in_specs=in_specs, out_specs=out_specs, check_vma=False)
```

profile of v0, /device:TPU:1, one launch (start us, length us, event | category | flops | bytes accessed | tf_op | source)
XLA Modules:
  0.0 331.4 jit_solution(16213828471275426308)
XLA Ops:
  7.2 0.0 all-gather.2.cloned.1.call-start
  7.2 1.1 fusion.20
  8.4 1.8 fusion.21
  10.2 0.0 all-gather.2.cloned.1.call-update
  10.2 0.0 reduce-scatter.5.cloned.1.call-start
  10.2 69.7 %all-gather.2.cloned.1.call-done = bf16[512,1152]{1,0:T(8,128)(2,1)} async-done(((bf16[128,1152]{1,0:T(8,128)(2,1)}), bf16[512,1152]{1,0:T(8,128)(2,1)}) %all-gather.2.cloned.1.call-update) | async-done | bytes 1179664 | tf_op jit(solution)/shard_map/all_gather | solution.py:42
  79.9 3.1 collective-permute-start
  84.3 0.1 fusion.14
  84.5 35.7 %collective-permute-done = bf16[512,1152]{1,0:T(8,128)(2,1)S(1)} collective-permute-done((bf16[512,1152]{1,0:T(8,128)(2,1)}, bf16[512,1152]{1,0:T(8,128)(2,1)S(1)}, u32[]{:S(2)}, u32[]{:S(2)}) %collective-permute-start) | collective-permute-done | bytes 1179680 | tf_op jit(solution)/shard_map/ppermute | solution.py:15
  120.1 0.6 fusion.13
  120.7 2.0 convolution_multiply_fusion
  122.7 0.0 reduce-scatter.3.cloned.1.call-start
  122.8 0.6 copy-done.3
  123.3 0.6 copy-done.2
  124.0 0.6 fusion.12
  124.6 1.9 convolution_multiply_fusion.1
  126.5 0.3 fusion.32
  126.9 92.5 %reduce-scatter.5.cloned.1.call-done = f32[128,1152]{1,0:T(8,128)} async-done(((f32[512,1152]{1,0:T(8,128)}), f32[128,1152]{1,0:T(8,128)}) %reduce-scatter.5.cloned.1.call-update) | async-done | bytes 589840 | tf_op jit(solution)/shard_map/reduce_scatter | solution.py:63
  219.4 6.4 %collective-permute-start.1 = (f32[128,1152]{1,0:T(8,128)}, f32[128,1152]{1,0:T(8,128)S(1)}, u32[]{:S(2)}, u32[]{:S(2)}) collective-permute-start(f32[128,1152]{1,0:T(8,128)} %reduce-scatter.5.cloned.1.call-done), channel_id=1, source_target_pairs={{0,1020},{4,0},{8,4},{12,8},{16,12},{20,16},{24,20},{28,24},{32,28... | collective-permute-start | bytes 1769480 | tf_op jit(solution)/shard_map/ppermute | solution.py:15
  225.9 0.4 fusion.19
  226.3 1.1 fusion.18
  227.4 95.2 %reduce-scatter.3.cloned.1.call-done = f32[128,1152]{1,0:T(8,128)} async-done(((f32[512,1152]{1,0:T(8,128)}), f32[128,1152]{1,0:T(8,128)}) %reduce-scatter.3.cloned.1.call-update) | async-done | bytes 589840 | tf_op jit(solution)/shard_map/reduce_scatter | solution.py:63
  322.6 1.2 fusion.25
  323.8 1.1 fusion.24
  (12 shorter events, 0.1 us)
Async XLA Ops:
  7.2 77.2 %copy-start = (bf16[128,1152]{1,0:T(8,128)(2,1)S(1)}, bf16[128,1152]{1,0:T(8,128)(2,1)}, u32[]{:S(2)}) copy-start(bf16[128,1152]{1,0:T(8,128)(2,1)} %param.5) | copy-start | bytes 884740
  7.2 72.8 %all-gather.2.cloned.1.call-start = ((), (), s32[]{:S(2)}) async-start(), calls=%async_computation.2 | async-start | bytes 1474560 | tf_op jit(solution)/shard_map/all_gather | solution.py:42
  10.2 209.2 %reduce-scatter.5.cloned.1.call-start = ((), (), s32[]{:S(2)}) async-start(), calls=%async_computation.4 | async-start | bytes 2949120 | tf_op jit(solution)/shard_map/reduce_scatter | solution.py:63
  79.9 40.2 %collective-permute-start = (bf16[512,1152]{1,0:T(8,128)(2,1)}, bf16[512,1152]{1,0:T(8,128)(2,1)S(1)}, u32[]{:S(2)}, u32[]{:S(2)}) collective-permute-start(bf16[512,1152]{1,0:T(8,128)(2,1)} %all-gather.2.cloned.1.call-done), channel_id=1, source_target_pairs={{0,4},{4,8},{8,12},{12,16},{16,20},{20,24},{24,28},{28,32},{32,36}... | collective-permute-start | bytes 3538952 | tf_op jit(solution)/shard_map/ppermute | solution.py:15
  122.7 0.7 copy-start.3
  122.7 1.3 copy-start.2
  122.7 199.8 %reduce-scatter.3.cloned.1.call-start = ((), (), s32[]{:S(2)}) async-start(), calls=%async_computation.3 | async-start | bytes 2949120 | tf_op jit(solution)/shard_map/reduce_scatter | solution.py:63
  219.4 103.2 %collective-permute-start.1 = (f32[128,1152]{1,0:T(8,128)}, f32[128,1152]{1,0:T(8,128)S(1)}, u32[]{:S(2)}, u32[]{:S(2)}) collective-permute-start(f32[128,1152]{1,0:T(8,128)} %reduce-scatter.5.cloned.1.call-done), channel_id=1, source_target_pairs={{0,1020},{4,0},{8,4},{12,8},{16,12},{20,16},{24,20},{28,24},{32,28... | collective-permute-start | bytes 1769480 | tf_op jit(solution)/shard_map/ppermute | solution.py:15
  226.3 96.3 %copy-start.1 = (bf16[128,1152]{1,0:T(8,128)(2,1)S(1)}, bf16[128,1152]{1,0:T(8,128)(2,1)}, u32[]{:S(2)}) copy-start(bf16[128,1152]{1,0:T(8,128)(2,1)} %param.6) | copy-start | bytes 884740
Sparse Core Ops, SparseCore 0:
  11.3 68.6 all-gather.1
  122.8 96.5 reduce-scatter.4
  223.5 98.9 reduce-scatter.2
where the time goes:
time: 332 us; the launch traced here: 331 us
  waiting for transfers between devices  293 us (88%)
  between operations  15.1 us (5%)
  starting transfers between devices  9.65 us (3%)
  other arithmetic  6.47 us (2%)
  matrix products  5.83 us (2%)
    reduce_scatter x2, waiting for transfers between devices, local(): lax.psum_scatter(text_term, 'group', scatter_dimension=0, tiled=True)  188 us
    all_gather x1, waiting for transfers between devices, local(): met_text = lax.all_gather(text_unit, 'group', axis=0, tiled=True)  69.7 us
    ppermute x2, waiting for transfers between devices, shifted(): return lax.ppermute(value, axis, pairs)  35.7 us
    ppermute x2, starting transfers between devices, shifted(): return lax.ppermute(value, axis, pairs)  9.53 us
  transfers between devices with their start and end apart: 5, of which 4 were waited for; matrix products, arithmetic and copies ran while one was open for 1% of the time, Pallas kernels for 0%

commit v1 on v0

v1 whole, which is shorter than its diff:
```python
import functools
import jax
import jax.numpy as jnp
from jax import lax
from jax.experimental import pallas as pl
from jax.experimental.pallas import tpu as pltpu
from jax.sharding import PartitionSpec as P

AXES = ("blk", "group")
norm_eps = 1e-06


def moved(value, steps, flip):
    blocks, groups = lax.axis_size("blk"), lax.axis_size("group")
    pairs = [
        (b * groups + g, ((b + steps) % blocks) * groups + (g ^ flip))
        for b in range(blocks)
        for g in range(groups)
    ]
    return lax.ppermute(value, AXES, pairs)


def unit_rows(values):
    wide = values.astype(jnp.float32)
    inverse = lax.rsqrt(jnp.sum(wide * wide, axis=-1, keepdims=True) + norm_eps)
    return (wide, inverse, (wide * inverse).astype(jnp.bfloat16))


def unit_backward(wide, inverse, upstream):
    inner = jnp.sum(wide * upstream, axis=-1, keepdims=True)
    return inverse * (upstream - inverse * inverse * wide * inner)


def dot_rows(a, b):
    return lax.dot_general(a, b, (((1,), (1,)), ((), ())), preferred_element_type=jnp.float32)


def gradient_terms(count, diagonal, final, *refs):
    scale_ref, bias_ref, image_ref, text_ref = refs[:4]
    refs = refs[4:]
    scale, bias = scale_ref[0], bias_ref[0]
    image_wide, image_inv, image_unit = unit_rows(image_ref[...])
    text_wide, text_inv, text_unit = unit_rows(text_ref[...])
    image_sum = text_sum = None

    def add(total, term):
        return term if total is None else total + term

    if diagonal:
        pos_ref, refs = refs[0], refs[1:]
        weights = jax.nn.sigmoid(scale * dot_rows(image_unit, text_unit) + bias)
        columns = lax.broadcasted_iota(jnp.int32, weights.shape, 1)
        weights = weights - (columns == pos_ref[...]).astype(jnp.float32)
        image_sum = jnp.dot(weights.astype(jnp.bfloat16), text_unit, preferred_element_type=jnp.float32)
        text_sum = jnp.dot(weights.T.astype(jnp.bfloat16), image_unit, preferred_element_type=jnp.float32)
    if not diagonal:
        image_sum, text_sum = refs[0][...], refs[1][...]
        refs = refs[2:]
    text_refs, image_refs, outs = refs[: count[0]], refs[count[0] : sum(count)], refs[sum(count) :]
    for met_ref in text_refs:
        met = unit_rows(met_ref[...])[2]
        weights = jax.nn.sigmoid(scale * dot_rows(image_unit, met) + bias)
        image_sum = image_sum + jnp.dot(weights.astype(jnp.bfloat16), met, preferred_element_type=jnp.float32)
    for met_ref in image_refs:
        met = unit_rows(met_ref[...])[2]
        weights = jax.nn.sigmoid(scale * dot_rows(text_unit, met) + bias)
        text_sum = text_sum + jnp.dot(weights.astype(jnp.bfloat16), met, preferred_element_type=jnp.float32)
    if final:
        image_sum = unit_backward(image_wide, image_inv, scale * image_sum)
        text_sum = unit_backward(text_wide, text_inv, scale * text_sum)
    outs[0][...] = image_sum
    outs[1][...] = text_sum


def terms(scale, bias, image, text, met_texts, met_images, positives=None, sums=None, final=False):
    smem = pl.BlockSpec(memory_space=pltpu.SMEM)
    vmem = pl.BlockSpec(memory_space=pltpu.VMEM)
    diagonal = positives is not None
    extra = [positives[:, None]] if diagonal else list(sums)
    operands = [image, text, *extra, *met_texts, *met_images]
    rows, width = image.shape
    out = jax.ShapeDtypeStruct((rows, width), jnp.float32)
    subs = len(met_texts) + len(met_images)
    return pl.pallas_call(
        functools.partial(gradient_terms, (len(met_texts), len(met_images)), diagonal, final),
        out_shape=(out, out),
        in_specs=[smem, smem] + [vmem] * len(operands),
        out_specs=(vmem, vmem),
        compiler_params=pltpu.CompilerParams(vmem_limit_bytes=40 * 1024 * 1024),
        cost_estimate=pl.CostEstimate(
            flops=4 * rows * rows * width * subs, bytes_accessed=2 * rows * width * (subs + 6), transcendentals=0
        ),
    )(scale, bias, *operands)


def local(image, text, positives, scale, bias):
    far_text = moved(text, 0, 2)
    far_image = moved(image, 0, 2)
    last_text = moved(text, 1, 0)
    next_image = moved(image, -1, 0)
    near = [text, last_text, image, next_image]
    twin = [moved(v, 0, 1) for v in near]
    sums = terms(
        scale, bias, image, text, [twin[0], last_text, twin[1]], [twin[2], next_image, twin[3]], positives=positives
    )
    far_last_text = moved(far_text, 1, 0)
    far_next_image = moved(far_image, -1, 0)
    far_text_twin = moved(far_text, 0, 1)
    far_image_twin = moved(far_image, 0, 1)
    sums = terms(scale, bias, image, text, [far_text, far_text_twin], [far_image, far_image_twin], sums=sums)
    far_last_twin = moved(far_last_text, 0, 1)
    far_next_twin = moved(far_next_image, 0, 1)
    return terms(
        scale,
        bias,
        image,
        text,
        [far_last_text, far_last_twin],
        [far_next_image, far_next_twin],
        sums=sums,
        final=True,
    )


def solution(mesh):
    in_specs = (P(AXES, None), P(AXES, None), P(AXES), P(), P())
    out_specs = (P(AXES, None), P(AXES, None))
    return jax.shard_map(local, mesh=mesh, in_specs=in_specs, out_specs=out_specs, check_vma=False)
```

time: 332 us -> 131 us (0.39)
  waiting for transfers between devices: 293 us -> 29.3 us
  starting transfers between devices: 9.65 us -> 85.9 us
  between operations: 15.1 us -> 2.15 us
  Pallas kernels: 0 us -> 8.86 us
  other arithmetic: 6.47 us -> 0 us
  matrix products: 5.83 us -> 0 us
    reduce_scatter x2 -> x0, waiting for transfers between devices: 188 us -> none  [local(): lax.psum_scatter(text_term, 'group', scatter_dimension=0, tiled=True)]
    ppermute x2 -> x14, starting transfers between devices: 9.53 us -> 85.9 us  [moved(): return lax.ppermute(value, AXES, pairs)]
    all_gather x1 -> x0, waiting for transfers between devices: 69.7 us -> none  [local(): met_text = lax.all_gather(text_unit, 'group', axis=0, tiled=True)]
    pallas_call x0 -> x3, Pallas kernels: none -> 8.86 us  [terms(): pl.pallas_call(functools.partial(gradient_terms, (len(met_texts), len(met...]
    ppermute x2 -> x14, waiting for transfers between devices: 35.7 us -> 29.3 us  [moved(): return lax.ppermute(value, AXES, pairs)]
    dot_general x6 -> x0, matrix products: 5.83 us -> none  [the longest x2 3.91 us: local(): lax.dot_general(coeff, image_unit, (((0,), (0,)), ((), ())), preferred_el...]
  transfers between devices with their start and end apart: 5 -> 14, of which waited for: 4 -> 2; matrix products, arithmetic and copies ran while one was open for 1% -> 1% of each run, Pallas kernels for 0% -> 4%
where the time goes in v1:
time: 131 us; the launch traced here: 130 us
  starting transfers between devices  85.9 us (66%)
  waiting for transfers between devices  29.3 us (22%)
  Pallas kernels  8.86 us (7%)
  local copies, waits for them, and re-layouts  4.15 us (3%)
  between operations  2.15 us (2%)
    ppermute x14, starting transfers between devices, moved(): return lax.ppermute(value, AXES, pairs)  85.9 us
    ppermute x14, waiting for transfers between devices, moved(): return lax.ppermute(value, AXES, pairs)  29.3 us
    pallas_call x3, Pallas kernels, terms(): pl.pallas_call(functools.partial(gradient_terms, (len(met_texts), len(met...  8.86 us
    unnamed x8, local copies, waits for them, and re-layouts  3.41 us
  transfers between devices with their start and end apart: 14, of which 2 were waited for; matrix products, arithmetic and copies ran while one was open for 1% of the time, Pallas kernels for 4%

profile of v1, /device:TPU:1, one launch (start us, length us, event | category | flops | bytes accessed | tf_op | source)
XLA Modules:
  0.0 130.4 jit_solution(1156223850824421644)
XLA Ops:
  0.6 4.0 %collective-permute-start.1 = (bf16[128,1152]{1,0:T(8,128)(2,1)}, bf16[128,1152]{1,0:T(8,128)(2,1)S(1)}, u32[]{:S(2)}, u32[]{:S(2)}) collective-permute-start(bf16[128,1152]{1,0:T(8,128)(2,1)} %refs_3_.5), channel_id=1, source_target_pairs={{0,4},{1,5},{2,6},{3,7},{4,8},{5,9},{6,10},{7,11},{8,12},{9,13},{1... | collective-permute-start | bytes 884744 | tf_op jit(solution)/shard_map/ppermute | solution.py:20
  4.6 20.0 %collective-permute-start.4 = (bf16[128,1152]{1,0:T(8,128)(2,1)}, bf16[128,1152]{1,0:T(8,128)(2,1)S(1)}, u32[]{:S(2)}, u32[]{:S(2)}) collective-permute-start(bf16[128,1152]{1,0:T(8,128)(2,1)} %refs_2_.5), channel_id=1, source_target_pairs={{0,1020},{1,1021},{2,1022},{3,1023},{4,0},{5,1},{6,2},{7,3},{8,4},... | collective-permute-start | bytes 884744 | tf_op jit(solution)/shard_map/ppermute | solution.py:20
  24.6 12.1 %collective-permute-start.6 = (bf16[128,1152]{1,0:T(8,128)(2,1)}, bf16[128,1152]{1,0:T(8,128)(2,1)S(1)}, u32[]{:S(2)}, u32[]{:S(2)}) collective-permute-start(bf16[128,1152]{1,0:T(8,128)(2,1)} %refs_3_.5), channel_id=1, source_target_pairs={{0,2},{1,3},{2,0},{3,1},{4,6},{5,7},{6,4},{7,5},{8,10},{9,11},{10,... | collective-permute-start | bytes 884744 | tf_op jit(solution)/shard_map/ppermute | solution.py:20
  36.7 1.9 %collective-permute-start.8 = (bf16[128,1152]{1,0:T(8,128)(2,1)}, bf16[128,1152]{1,0:T(8,128)(2,1)S(1)}, u32[]{:S(2)}, u32[]{:S(2)}) collective-permute-start(bf16[128,1152]{1,0:T(8,128)(2,1)} %refs_2_.5), channel_id=1, source_target_pairs={{0,2},{1,3},{2,0},{3,1},{4,6},{5,7},{6,4},{7,5},{8,10},{9,11},{10,... | collective-permute-start | bytes 884744 | tf_op jit(solution)/shard_map/ppermute | solution.py:20
  38.6 9.4 %collective-permute-start = (bf16[128,1152]{1,0:T(8,128)(2,1)}, bf16[128,1152]{1,0:T(8,128)(2,1)S(1)}, u32[]{:S(2)}, u32[]{:S(2)}) collective-permute-start(bf16[128,1152]{1,0:T(8,128)(2,1)} %refs_3_.5), channel_id=1, source_target_pairs={{0,1},{1,0},{2,3},{3,2},{4,5},{5,4},{6,7},{7,6},{8,9},{9,8},{10,11... | collective-permute-start | bytes 884744 | tf_op jit(solution)/shard_map/ppermute | solution.py:20
  48.0 1.9 %collective-permute-start.3 = (bf16[128,1152]{1,0:T(8,128)(2,1)}, bf16[128,1152]{1,0:T(8,128)(2,1)S(1)}, u32[]{:S(2)}, u32[]{:S(2)}) collective-permute-start(bf16[128,1152]{1,0:T(8,128)(2,1)} %refs_2_.5), channel_id=1, source_target_pairs={{0,1},{1,0},{2,3},{3,2},{4,5},{5,4},{6,7},{7,6},{8,9},{9,8},{10,11... | collective-permute-start | bytes 884744 | tf_op jit(solution)/shard_map/ppermute | solution.py:20
  49.9 10.5 %collective-permute-start.2 = (bf16[128,1152]{1,0:T(8,128)(2,1)S(1)}, bf16[128,1152]{1,0:T(8,128)(2,1)S(1)}, u32[]{:S(2)}, u32[]{:S(2)}) collective-permute-start(bf16[128,1152]{1,0:T(8,128)(2,1)S(1)} %collective-permute-done.1.refs_6_), channel_id=1, source_target_pairs={{0,1},{1,0},{2,3},{3,2},{4,5},{5,4},{6,7},{7,6},{8,9},{9,8},{10,11... | collective-permute-start | bytes 884744 | tf_op jit(solution)/shard_map/ppermute | solution.py:20
  60.5 24.8 %collective-permute-done.6.refs_6_ = bf16[128,1152]{1,0:T(8,128)(2,1)S(1)} collective-permute-done((bf16[128,1152]{1,0:T(8,128)(2,1)}, bf16[128,1152]{1,0:T(8,128)(2,1)S(1)}, u32[]{:S(2)}, u32[]{:S(2)}) %collective-permute-start.6) | collective-permute-done | bytes 294944 | tf_op jit(solution)/shard_map/ppermute | solution.py:20
  85.3 1.9 %collective-permute-start.10 = (bf16[128,1152]{1,0:T(8,128)(2,1)S(1)}, bf16[128,1152]{1,0:T(8,128)(2,1)S(1)}, u32[]{:S(2)}, u32[]{:S(2)}) collective-permute-start(bf16[128,1152]{1,0:T(8,128)(2,1)S(1)} %collective-permute-done.6.refs_6_), channel_id=1, source_target_pairs={{0,4},{1,5},{2,6},{3,7},{4,8},{5,9},{6,10},{7,11},{8,12},{9,13},{1... | collective-permute-start | bytes 884744 | tf_op jit(solution)/shard_map/ppermute | solution.py:20
  87.2 4.4 %collective-permute-done.8.refs_8_ = bf16[128,1152]{1,0:T(8,128)(2,1)S(1)} collective-permute-done((bf16[128,1152]{1,0:T(8,128)(2,1)}, bf16[128,1152]{1,0:T(8,128)(2,1)S(1)}, u32[]{:S(2)}, u32[]{:S(2)}) %collective-permute-start.8) | collective-permute-done | bytes 294944 | tf_op jit(solution)/shard_map/ppermute | solution.py:20
  91.6 9.8 %collective-permute-start.12 = (bf16[128,1152]{1,0:T(8,128)(2,1)S(1)}, bf16[128,1152]{1,0:T(8,128)(2,1)S(1)}, u32[]{:S(2)}, u32[]{:S(2)}) collective-permute-start(bf16[128,1152]{1,0:T(8,128)(2,1)S(1)} %collective-permute-done.8.refs_8_), channel_id=1, source_target_pairs={{0,1020},{1,1021},{2,1022},{3,1023},{4,0},{5,1},{6,2},{7,3},{8,4},... | collective-permute-start | bytes 884744 | tf_op jit(solution)/shard_map/ppermute | solution.py:20
  101.4 5.8 %collective-permute-start.5 = (bf16[128,1152]{1,0:T(8,128)(2,1)S(1)}, bf16[128,1152]{1,0:T(8,128)(2,1)S(1)}, u32[]{:S(2)}, u32[]{:S(2)}) collective-permute-start(bf16[128,1152]{1,0:T(8,128)(2,1)S(1)} %collective-permute-done.4.refs_9_), channel_id=1, source_target_pairs={{0,1},{1,0},{2,3},{3,2},{4,5},{5,4},{6,7},{7,6},{8,9},{9,8},{10,11... | collective-permute-start | bytes 884744 | tf_op jit(solution)/shard_map/ppermute | solution.py:20
  107.3 1.9 %collective-permute-start.7 = (bf16[128,1152]{1,0:T(8,128)(2,1)S(1)}, bf16[128,1152]{1,0:T(8,128)(2,1)S(1)}, u32[]{:S(2)}, u32[]{:S(2)}) collective-permute-start(bf16[128,1152]{1,0:T(8,128)(2,1)S(1)} %collective-permute-done.6.refs_6_), channel_id=1, source_target_pairs={{0,1},{1,0},{2,3},{3,2},{4,5},{5,4},{6,7},{7,6},{8,9},{9,8},{10,11... | collective-permute-start | bytes 884744 | tf_op jit(solution)/shard_map/ppermute | solution.py:20
  109.2 2.4 %collective-permute-start.9 = (bf16[128,1152]{1,0:T(8,128)(2,1)S(1)}, bf16[128,1152]{1,0:T(8,128)(2,1)}, u32[]{:S(2)}, u32[]{:S(2)}) collective-permute-start(bf16[128,1152]{1,0:T(8,128)(2,1)S(1)} %collective-permute-done.8.refs_8_), channel_id=1, source_target_pairs={{0,1},{1,0},{2,3},{3,2},{4,5},{5,4},{6,7},{7,6},{8,9},{9,8},{10,11... | collective-permute-start | bytes 884744 | tf_op jit(solution)/shard_map/ppermute | solution.py:20
  111.6 1.9 %collective-permute-start.11 = (bf16[128,1152]{1,0:T(8,128)(2,1)S(1)}, bf16[128,1152]{1,0:T(8,128)(2,1)S(1)}, u32[]{:S(2)}, u32[]{:S(2)}) collective-permute-start(bf16[128,1152]{1,0:T(8,128)(2,1)S(1)} %collective-permute-done.10.refs_6_), channel_id=1, source_target_pairs={{0,1},{1,0},{2,3},{3,2},{4,5},{5,4},{6,7},{7,6},{8,9},{9,8},{10,11... | collective-permute-start | bytes 884744 | tf_op jit(solution)/shard_map/ppermute | solution.py:20
  113.6 2.4 %collective-permute-start.13 = (bf16[128,1152]{1,0:T(8,128)(2,1)S(1)}, bf16[128,1152]{1,0:T(8,128)(2,1)}, u32[]{:S(2)}, u32[]{:S(2)}) collective-permute-start(bf16[128,1152]{1,0:T(8,128)(2,1)S(1)} %collective-permute-done.12.refs_8_), channel_id=1, source_target_pairs={{0,1},{1,0},{2,3},{3,2},{4,5},{5,4},{6,7},{7,6},{8,9},{9,8},{10,11... | collective-permute-start | bytes 884744 | tf_op jit(solution)/shard_map/ppermute | solution.py:20
  117.3 0.6 copy-done.3
  117.9 0.7 copy.7.refs_4_
  118.7 1.0 copy-done
  119.6 1.0 copy-done.1
  120.6 0.8 copy-done.2
  121.4 2.5 %shard_map.68 = (f32[128,1152]{1,0:T(8,128)S(1)}, f32[128,1152]{1,0:T(8,128)S(1)}) custom-call(f32[1]{0:T(128)S(6)} %copy.8.refs_0_, f32[1]{0:T(128)S(6)} %copy.9.refs_1_, bf16[128,1152]{1,0:T(8,128)(2,1)S(1)} %copy-done, bf16[128,1152]{1,0:T(8,128)(2,1)S(1)} %copy-done.1, s32[128,1]{1,0:T(8,128)S(1)} %copy-done.2, ...), custom_call_target="tpu_custom_call" | custom-call | flops 452984832 | bytes 3538944 | tf_op jit(solution)/shard_map/pallas_call | solution.py:84
  124.0 2.6 %shard_map.69 = (f32[128,1152]{1,0:T(8,128)S(1)}, f32[128,1152]{1,0:T(8,128)S(1)}) custom-call(f32[1]{0:T(128)S(6)} %copy.8.refs_0_, f32[1]{0:T(128)S(6)} %copy.9.refs_1_, bf16[128,1152]{1,0:T(8,128)(2,1)S(1)} %copy-done, bf16[128,1152]{1,0:T(8,128)(2,1)S(1)} %copy-done.1, f32[128,1152]{1,0:T(8,128)S(1)} %get-tuple-element.6.refs_4_, ...), custom_call_target="tpu_custom_call" | custom-call | flops 301989888 | bytes 2949120 | tf_op jit(solution)/shard_map/pallas_call | solution.py:84
  126.7 3.7 %shard_map.70 = (f32[128,1152]{1,0:T(8,128)}, f32[128,1152]{1,0:T(8,128)}) custom-call(f32[1]{0:T(128)S(6)} %copy.8.refs_0_, f32[1]{0:T(128)S(6)} %copy.9.refs_1_, bf16[128,1152]{1,0:T(8,128)(2,1)S(1)} %copy-done, bf16[128,1152]{1,0:T(8,128)(2,1)S(1)} %copy-done.1, f32[128,1152]{1,0:T(8,128)S(1)} %get-tuple-element.8.refs_4_, ...), custom_call_target="tpu_custom_call" | custom-call | flops 301989888 | bytes 2949120 | tf_op jit(solution)/shard_map/pallas_call | solution.py:84
  (16 shorter events, 0.0 us)
Async XLA Ops:
  0.6 47.3 %collective-permute-start.1 = (bf16[128,1152]{1,0:T(8,128)(2,1)}, bf16[128,1152]{1,0:T(8,128)(2,1)S(1)}, u32[]{:S(2)}, u32[]{:S(2)}) collective-permute-start(bf16[128,1152]{1,0:T(8,128)(2,1)} %refs_3_.5), channel_id=1, source_target_pairs={{0,4},{1,5},{2,6},{3,7},{4,8},{5,9},{6,10},{7,11},{8,12},{9,13},{1... | collective-permute-start | bytes 884744 | tf_op jit(solution)/shard_map/ppermute | solution.py:20
  4.6 45.3 %collective-permute-start.4 = (bf16[128,1152]{1,0:T(8,128)(2,1)}, bf16[128,1152]{1,0:T(8,128)(2,1)S(1)}, u32[]{:S(2)}, u32[]{:S(2)}) collective-permute-start(bf16[128,1152]{1,0:T(8,128)(2,1)} %refs_2_.5), channel_id=1, source_target_pairs={{0,1020},{1,1021},{2,1022},{3,1023},{4,0},{5,1},{6,2},{7,3},{8,4},... | collective-permute-start | bytes 884744 | tf_op jit(solution)/shard_map/ppermute | solution.py:20
  24.6 60.7 %collective-permute-start.6 = (bf16[128,1152]{1,0:T(8,128)(2,1)}, bf16[128,1152]{1,0:T(8,128)(2,1)S(1)}, u32[]{:S(2)}, u32[]{:S(2)}) collective-permute-start(bf16[128,1152]{1,0:T(8,128)(2,1)} %refs_3_.5), channel_id=1, source_target_pairs={{0,2},{1,3},{2,0},{3,1},{4,6},{5,7},{6,4},{7,5},{8,10},{9,11},{10,... | collective-permute-start | bytes 884744 | tf_op jit(solution)/shard_map/ppermute | solution.py:20
  36.7 54.9 %collective-permute-start.8 = (bf16[128,1152]{1,0:T(8,128)(2,1)}, bf16[128,1152]{1,0:T(8,128)(2,1)S(1)}, u32[]{:S(2)}, u32[]{:S(2)}) collective-permute-start(bf16[128,1152]{1,0:T(8,128)(2,1)} %refs_2_.5), channel_id=1, source_target_pairs={{0,2},{1,3},{2,0},{3,1},{4,6},{5,7},{6,4},{7,5},{8,10},{9,11},{10,... | collective-permute-start | bytes 884744 | tf_op jit(solution)/shard_map/ppermute | solution.py:20
  38.6 62.8 %collective-permute-start = (bf16[128,1152]{1,0:T(8,128)(2,1)}, bf16[128,1152]{1,0:T(8,128)(2,1)S(1)}, u32[]{:S(2)}, u32[]{:S(2)}) collective-permute-start(bf16[128,1152]{1,0:T(8,128)(2,1)} %refs_3_.5), channel_id=1, source_target_pairs={{0,1},{1,0},{2,3},{3,2},{4,5},{5,4},{6,7},{7,6},{8,9},{9,8},{10,11... | collective-permute-start | bytes 884744 | tf_op jit(solution)/shard_map/ppermute | solution.py:20
  48.0 59.3 %collective-permute-start.3 = (bf16[128,1152]{1,0:T(8,128)(2,1)}, bf16[128,1152]{1,0:T(8,128)(2,1)S(1)}, u32[]{:S(2)}, u32[]{:S(2)}) collective-permute-start(bf16[128,1152]{1,0:T(8,128)(2,1)} %refs_2_.5), channel_id=1, source_target_pairs={{0,1},{1,0},{2,3},{3,2},{4,5},{5,4},{6,7},{7,6},{8,9},{9,8},{10,11... | collective-permute-start | bytes 884744 | tf_op jit(solution)/shard_map/ppermute | solution.py:20
  49.9 59.3 %collective-permute-start.2 = (bf16[128,1152]{1,0:T(8,128)(2,1)S(1)}, bf16[128,1152]{1,0:T(8,128)(2,1)S(1)}, u32[]{:S(2)}, u32[]{:S(2)}) collective-permute-start(bf16[128,1152]{1,0:T(8,128)(2,1)S(1)} %collective-permute-done.1.refs_6_), channel_id=1, source_target_pairs={{0,1},{1,0},{2,3},{3,2},{4,5},{5,4},{6,7},{7,6},{8,9},{9,8},{10,11... | collective-permute-start | bytes 884744 | tf_op jit(solution)/shard_map/ppermute | solution.py:20
  85.3 26.3 %collective-permute-start.10 = (bf16[128,1152]{1,0:T(8,128)(2,1)S(1)}, bf16[128,1152]{1,0:T(8,128)(2,1)S(1)}, u32[]{:S(2)}, u32[]{:S(2)}) collective-permute-start(bf16[128,1152]{1,0:T(8,128)(2,1)S(1)} %collective-permute-done.6.refs_6_), channel_id=1, source_target_pairs={{0,4},{1,5},{2,6},{3,7},{4,8},{5,9},{6,10},{7,11},{8,12},{9,13},{1... | collective-permute-start | bytes 884744 | tf_op jit(solution)/shard_map/ppermute | solution.py:20
  91.6 22.0 %collective-permute-start.12 = (bf16[128,1152]{1,0:T(8,128)(2,1)S(1)}, bf16[128,1152]{1,0:T(8,128)(2,1)S(1)}, u32[]{:S(2)}, u32[]{:S(2)}) collective-permute-start(bf16[128,1152]{1,0:T(8,128)(2,1)S(1)} %collective-permute-done.8.refs_8_), channel_id=1, source_target_pairs={{0,1020},{1,1021},{2,1022},{3,1023},{4,0},{5,1},{6,2},{7,3},{8,4},... | collective-permute-start | bytes 884744 | tf_op jit(solution)/shard_map/ppermute | solution.py:20
  101.4 17.3 %collective-permute-start.5 = (bf16[128,1152]{1,0:T(8,128)(2,1)S(1)}, bf16[128,1152]{1,0:T(8,128)(2,1)S(1)}, u32[]{:S(2)}, u32[]{:S(2)}) collective-permute-start(bf16[128,1152]{1,0:T(8,128)(2,1)S(1)} %collective-permute-done.4.refs_9_), channel_id=1, source_target_pairs={{0,1},{1,0},{2,3},{3,2},{4,5},{5,4},{6,7},{7,6},{8,9},{9,8},{10,11... | collective-permute-start | bytes 884744 | tf_op jit(solution)/shard_map/ppermute | solution.py:20
  107.3 16.7 %collective-permute-start.7 = (bf16[128,1152]{1,0:T(8,128)(2,1)S(1)}, bf16[128,1152]{1,0:T(8,128)(2,1)S(1)}, u32[]{:S(2)}, u32[]{:S(2)}) collective-permute-start(bf16[128,1152]{1,0:T(8,128)(2,1)S(1)} %collective-permute-done.6.refs_6_), channel_id=1, source_target_pairs={{0,1},{1,0},{2,3},{3,2},{4,5},{5,4},{6,7},{7,6},{8,9},{9,8},{10,11... | collective-permute-start | bytes 884744 | tf_op jit(solution)/shard_map/ppermute | solution.py:20
  109.2 14.8 %collective-permute-start.9 = (bf16[128,1152]{1,0:T(8,128)(2,1)S(1)}, bf16[128,1152]{1,0:T(8,128)(2,1)}, u32[]{:S(2)}, u32[]{:S(2)}) collective-permute-start(bf16[128,1152]{1,0:T(8,128)(2,1)S(1)} %collective-permute-done.8.refs_8_), channel_id=1, source_target_pairs={{0,1},{1,0},{2,3},{3,2},{4,5},{5,4},{6,7},{7,6},{8,9},{9,8},{10,11... | collective-permute-start | bytes 884744 | tf_op jit(solution)/shard_map/ppermute | solution.py:20
  111.6 15.0 %collective-permute-start.11 = (bf16[128,1152]{1,0:T(8,128)(2,1)S(1)}, bf16[128,1152]{1,0:T(8,128)(2,1)S(1)}, u32[]{:S(2)}, u32[]{:S(2)}) collective-permute-start(bf16[128,1152]{1,0:T(8,128)(2,1)S(1)} %collective-permute-done.10.refs_6_), channel_id=1, source_target_pairs={{0,1},{1,0},{2,3},{3,2},{4,5},{5,4},{6,7},{7,6},{8,9},{9,8},{10,11... | collective-permute-start | bytes 884744 | tf_op jit(solution)/shard_map/ppermute | solution.py:20
  113.6 13.1 %collective-permute-start.13 = (bf16[128,1152]{1,0:T(8,128)(2,1)S(1)}, bf16[128,1152]{1,0:T(8,128)(2,1)}, u32[]{:S(2)}, u32[]{:S(2)}) collective-permute-start(bf16[128,1152]{1,0:T(8,128)(2,1)S(1)} %collective-permute-done.12.refs_8_), channel_id=1, source_target_pairs={{0,1},{1,0},{2,3},{3,2},{4,5},{5,4},{6,7},{7,6},{8,9},{9,8},{10,11... | collective-permute-start | bytes 884744 | tf_op jit(solution)/shard_map/ppermute | solution.py:20
  117.3 0.7 copy-start.3
  118.7 1.0 copy-start
  119.6 1.0 copy-start.1
  120.6 0.8 copy-start.2

commit v2 on v1

--- a/solution.py
+++ b/solution.py
@@ -56,13 +56,19 @@
     if not diagonal:
         image_sum, text_sum = refs[0][...], refs[1][...]
         refs = refs[2:]
-    text_refs, image_refs, outs = refs[: count[0]], refs[count[0] : sum(count)], refs[sum(count) :]
-    for met_ref in text_refs:
-        met = unit_rows(met_ref[...])[2]
+    rows = image_ref.shape[0]
+    texts, images, both = count
+    text_blocks = [(ref, 0) for ref in refs[:texts]]
+    image_blocks = [(ref, 0) for ref in refs[texts : texts + images]]
+    text_blocks += [(ref, 0) for ref in refs[texts + images : sum(count)]]
+    image_blocks += [(ref, rows) for ref in refs[texts + images : sum(count)]]
+    outs = refs[sum(count) :]
+    for met_ref, start in text_blocks:
+        met = unit_rows(met_ref[pl.ds(start, rows), :])[2]
         weights = jax.nn.sigmoid(scale * dot_rows(image_unit, met) + bias)
         image_sum = image_sum + jnp.dot(weights.astype(jnp.bfloat16), met, preferred_element_type=jnp.float32)
-    for met_ref in image_refs:
-        met = unit_rows(met_ref[...])[2]
+    for met_ref, start in image_blocks:
+        met = unit_rows(met_ref[pl.ds(start, rows), :])[2]
         weights = jax.nn.sigmoid(scale * dot_rows(text_unit, met) + bias)
         text_sum = text_sum + jnp.dot(weights.astype(jnp.bfloat16), met, preferred_element_type=jnp.float32)
     if final:
@@ -72,17 +78,17 @@
     outs[1][...] = text_sum
 
 
-def terms(scale, bias, image, text, met_texts, met_images, positives=None, sums=None, final=False):
+def terms(scale, bias, image, text, met_texts, met_images, met_both, positives=None, sums=None, final=False):
     smem = pl.BlockSpec(memory_space=pltpu.SMEM)
     vmem = pl.BlockSpec(memory_space=pltpu.VMEM)
     diagonal = positives is not None
     extra = [positives[:, None]] if diagonal else list(sums)
-    operands = [image, text, *extra, *met_texts, *met_images]
+    operands = [image, text, *extra, *met_texts, *met_images, *met_both]
     rows, width = image.shape
     out = jax.ShapeDtypeStruct((rows, width), jnp.float32)
-    subs = len(met_texts) + len(met_images)
+    subs = len(met_texts) + len(met_images) + 2 * len(met_both)
     return pl.pallas_call(
-        functools.partial(gradient_terms, (len(met_texts), len(met_images)), diagonal, final),
+        functools.partial(gradient_terms, (len(met_texts), len(met_images), len(met_both)), diagonal, final),
         out_shape=(out, out),
         in_specs=[smem, smem] + [vmem] * len(operands),
         out_specs=(vmem, vmem),
@@ -93,32 +99,44 @@
     )(scale, bias, *operands)
 
 
+RUN = 32
+
+
+def moved_block(value, steps):
+    blocks, groups = lax.axis_size("blk"), lax.axis_size("group")
+    pairs = []
+    for b in range(blocks):
+        to = (b + steps) % blocks
+        flip = 0 if b // RUN == to // RUN else groups // 2
+        pairs += [(b * groups + g, to * groups + (g ^ flip)) for g in range(groups)]
+    return lax.ppermute(value, AXES, pairs)
+
+
+def moved_half(value):
+    return moved(value, 0, lax.axis_size("group") // 2)
+
+
+def moved_core(value):
+    return moved(value, 0, 1)
+
+
 def local(image, text, positives, scale, bias):
-    far_text = moved(text, 0, 2)
-    far_image = moved(image, 0, 2)
-    last_text = moved(text, 1, 0)
-    next_image = moved(image, -1, 0)
-    near = [text, last_text, image, next_image]
-    twin = [moved(v, 0, 1) for v in near]
-    sums = terms(
-        scale, bias, image, text, [twin[0], last_text, twin[1]], [twin[2], next_image, twin[3]], positives=positives
-    )
-    far_last_text = moved(far_text, 1, 0)
-    far_next_image = moved(far_image, -1, 0)
-    far_text_twin = moved(far_text, 0, 1)
-    far_image_twin = moved(far_image, 0, 1)
-    sums = terms(scale, bias, image, text, [far_text, far_text_twin], [far_image, far_image_twin], sums=sums)
-    far_last_twin = moved(far_last_text, 0, 1)
-    far_next_twin = moved(far_next_image, 0, 1)
+    rows = text.shape[0]
+    own = jnp.concatenate([text, image])
+    far = moved_half(own)
+    last_text = moved_block(text, 1)
+    next_image = moved_block(image, -1)
+    twin = moved_core(own)
+    sums = terms(scale, bias, image, text, [], [], [twin], positives=positives)
+    far, last_text, next_image, sums = lax.optimization_barrier((far, last_text, next_image, sums))
+    far_last_text = moved_block(far[:rows], 1)
+    far_next_image = moved_block(far[rows:], -1)
+    far_twin = moved_core(far)
+    moved_twin = moved_core(jnp.concatenate([last_text, next_image]))
+    sums = terms(scale, bias, image, text, [last_text], [next_image], [far, far_twin, moved_twin], sums=sums)
+    far_moved_twin = moved_core(jnp.concatenate([far_last_text, far_next_image]))
     return terms(
-        scale,
-        bias,
-        image,
-        text,
-        [far_last_text, far_last_twin],
-        [far_next_image, far_next_twin],
-        sums=sums,
-        final=True,
+        scale, bias, image, text, [far_last_text], [far_next_image], [far_moved_twin], sums=sums, final=True
     )
 
 

time: 131 us -> 112 us (0.85)
  starting transfers between devices: 85.9 us -> 52.3 us
  waiting for transfers between devices: 29.3 us -> 49.2 us
  local copies, waits for them, and re-layouts: 4.15 us -> 1.27 us
  Pallas kernels: 8.86 us -> 6.9 us
    ppermute x14 -> x5, starting transfers between devices: 85.9 us -> 30.9 us  [moved(): return lax.ppermute(value, AXES, pairs)]
    ppermute x0 -> x4, waiting for transfers between devices: none -> 49.2 us  [moved_block(): return lax.ppermute(value, AXES, pairs)]
    ppermute x14 -> x5, waiting for transfers between devices: 29.3 us -> 0.01 us  [moved(): return lax.ppermute(value, AXES, pairs)]
    ppermute x0 -> x4, starting transfers between devices: none -> 21.4 us  [moved_block(): return lax.ppermute(value, AXES, pairs)]
    unnamed x8 -> x7, local copies, waits for them, and re-layouts: 3.41 us -> 1.08 us
    pallas_call x3, Pallas kernels: 8.86 us -> 6.9 us  [terms(): pl.pallas_call(functools.partial(gradient_terms, (len(met_texts), len(met...]
  transfers between devices with their start and end apart: 14 -> 9, of which waited for: 2 -> 2; matrix products, arithmetic and copies ran while one was open for 1% -> 0% of each run, Pallas kernels for 4% -> 4%
where the time goes in v2:
time: 112 us
  starting transfers between devices  52.3 us (47%)
  waiting for transfers between devices  49.2 us (44%)
  Pallas kernels  6.9 us (6%)
  between operations  2.1 us (2%)
  local copies, waits for them, and re-layouts  1.27 us (1%)
    ppermute x4, waiting for transfers between devices, moved_block(): return lax.ppermute(value, AXES, pairs)  49.2 us
    ppermute x5, starting transfers between devices, moved(): return lax.ppermute(value, AXES, pairs)  30.9 us
    ppermute x4, starting transfers between devices, moved_block(): return lax.ppermute(value, AXES, pairs)  21.4 us
    pallas_call x3, Pallas kernels, terms(): pl.pallas_call(functools.partial(gradient_terms, (len(met_texts), len(met...  6.9 us
  transfers between devices with their start and end apart: 9, of which 2 were waited for; matrix products, arithmetic and copies ran while one was open for 0% of the time, Pallas kernels for 4%

profile of v2, /device:TPU:1, one launch (start us, length us, event | category | flops | bytes accessed | tf_op | source)
XLA Modules:
  0.0 111.9 jit_solution(14111501018896217104)
XLA Ops:
  0.7 1.0 constant_dynamic-update-slice_fusion.1
  1.7 0.0 copy-done
  1.8 16.1 %collective-permute-start.3 = (bf16[256,1152]{1,0:T(8,128)(2,1)S(1)}, bf16[256,1152]{1,0:T(8,128)(2,1)S(1)}, u32[]{:S(2)}, u32[]{:S(2)}) collective-permute-start(bf16[256,1152]{1,0:T(8,128)(2,1)S(1)} %constant_dynamic-update-slice_fusion), channel_id=1, source_target_pairs={{0,1},{1,0},{2,3},{3,2},{4,5},{5,4},{6,7},{7,6},{8,9},{9,8},{10,11... | collective-permute-start | bytes 1769480 | tf_op jit(solution)/shard_map/ppermute | solution.py:20
  17.8 6.4 %collective-permute-start = (bf16[256,1152]{1,0:T(8,128)(2,1)S(1)}, bf16[256,1152]{1,0:T(8,128)(2,1)S(1)}, u32[]{:S(2)}, u32[]{:S(2)}) collective-permute-start(bf16[256,1152]{1,0:T(8,128)(2,1)S(1)} %constant_dynamic-update-slice_fusion), channel_id=1, source_target_pairs={{0,2},{1,3},{2,0},{3,1},{4,6},{5,7},{6,4},{7,5},{8,10},{9,11},{10,... | collective-permute-start | bytes 1769480 | tf_op jit(solution)/shard_map/ppermute | solution.py:20
  24.3 3.1 %collective-permute-start.1 = (bf16[128,1152]{1,0:T(8,128)(2,1)S(1)}, bf16[128,1152]{1,0:T(8,128)(2,1)S(1)}, u32[]{:S(2)}, u32[]{:S(2)}) collective-permute-start(bf16[128,1152]{1,0:T(8,128)(2,1)S(1)} %copy-done.1), channel_id=1, source_target_pairs={{0,4},{1,5},{2,6},{3,7},{4,8},{5,9},{6,10},{7,11},{8,12},{9,13},{1... | collective-permute-start | bytes 884744 | tf_op jit(solution)/shard_map/ppermute | solution.py:112
  27.4 7.6 %collective-permute-start.2 = (bf16[128,1152]{1,0:T(8,128)(2,1)S(1)}, bf16[128,1152]{1,0:T(8,128)(2,1)S(1)}, u32[]{:S(2)}, u32[]{:S(2)}) collective-permute-start(bf16[128,1152]{1,0:T(8,128)(2,1)S(1)} %copy-done), channel_id=1, source_target_pairs={{0,1022},{1,1023},{2,1020},{3,1021},{4,0},{5,1},{6,2},{7,3},{8,4},... | collective-permute-start | bytes 884744 | tf_op jit(solution)/shard_map/ppermute | solution.py:112
  36.3 0.1 copy.7.refs_4_
  36.4 0.0 collective-permute-done.3.refs_5_
  36.4 1.3 %shard_map.68 = (f32[128,1152]{1,0:T(8,128)S(1)}, f32[128,1152]{1,0:T(8,128)S(1)}) custom-call(f32[1]{0:T(128)S(6)} %copy.9.refs_0_, f32[1]{0:T(128)S(6)} %copy.10.refs_1_, bf16[128,1152]{1,0:T(8,128)(2,1)S(1)} %copy-done, bf16[128,1152]{1,0:T(8,128)(2,1)S(1)} %copy-done.1, s32[128,1]{1,0:T(8,128)S(1)} %copy.7.refs_4_, ...), custom_call_target="tpu_custom_call" | custom-call | flops 150994944 | bytes 2359296 | tf_op jit(solution)/shard_map/pallas_call | solution.py:90
  37.7 48.5 %collective-permute-done.1.refs_6_ = bf16[128,1152]{1,0:T(8,128)(2,1)S(1)} collective-permute-done((bf16[128,1152]{1,0:T(8,128)(2,1)S(1)}, bf16[128,1152]{1,0:T(8,128)(2,1)S(1)}, u32[]{:S(2)}, u32[]{:S(2)}) %collective-permute-start.1) | collective-permute-done | bytes 294944 | tf_op jit(solution)/shard_map/ppermute | solution.py:112
  86.2 0.0 collective-permute-done.2.refs_7_
  86.3 0.0 collective-permute-done.refs_8_
  86.3 1.9 %collective-permute-start.6 = (bf16[128,1152]{1,0:T(8,128)(2,1)S(1)}, bf16[128,1152]{1,0:T(8,128)(2,1)S(1)}, u32[]{:S(2)}, u32[]{:S(2)}) collective-permute-start(bf16[128,1152]{1,0:T(8,128)(2,1)S(1)} %get-tuple-element.21), channel_id=1, source_target_pairs={{0,4},{1,5},{2,6},{3,7},{4,8},{5,9},{6,10},{7,11},{8,12},{9,13},{1... | collective-permute-start | bytes 884744 | tf_op jit(solution)/shard_map/ppermute | solution.py:112
  88.2 8.8 %collective-permute-start.7 = (bf16[128,1152]{1,0:T(8,128)(2,1)S(1)}, bf16[128,1152]{1,0:T(8,128)(2,1)S(1)}, u32[]{:S(2)}, u32[]{:S(2)}) collective-permute-start(bf16[128,1152]{1,0:T(8,128)(2,1)S(1)} %get-tuple-element.20), channel_id=1, source_target_pairs={{0,1022},{1,1023},{2,1020},{3,1021},{4,0},{5,1},{6,2},{7,3},{8,4},... | collective-permute-start | bytes 884744 | tf_op jit(solution)/shard_map/ppermute | solution.py:112
  97.0 2.9 %collective-permute-start.4 = (bf16[256,1152]{1,0:T(8,128)(2,1)S(1)}, bf16[256,1152]{1,0:T(8,128)(2,1)S(1)}, u32[]{:S(2)}, u32[]{:S(2)}) collective-permute-start(bf16[256,1152]{1,0:T(8,128)(2,1)S(1)} %collective-permute-done.refs_8_), channel_id=1, source_target_pairs={{0,1},{1,0},{2,3},{3,2},{4,5},{5,4},{6,7},{7,6},{8,9},{9,8},{10,11... | collective-permute-start | bytes 1769480 | tf_op jit(solution)/shard_map/ppermute | solution.py:20
  100.0 1.9 %collective-permute-start.5 = (bf16[256,1152]{1,0:T(8,128)(2,1)S(1)}, bf16[256,1152]{1,0:T(8,128)(2,1)S(1)}, u32[]{:S(2)}, u32[]{:S(2)}) collective-permute-start(bf16[256,1152]{1,0:T(8,128)(2,1)S(1)} %pad_maximum_fusion), channel_id=1, source_target_pairs={{0,1},{1,0},{2,3},{3,2},{4,5},{5,4},{6,7},{7,6},{8,9},{9,8},{10,11... | collective-permute-start | bytes 1769480 | tf_op jit(solution)/shard_map/ppermute | solution.py:20
  102.0 0.0 collective-permute-done.6.refs_6_
  102.0 0.6 collective-permute-done.7.refs_7_
  102.7 3.5 %collective-permute-start.8 = (bf16[256,1152]{1,0:T(8,128)(2,1)S(1)}, bf16[256,1152]{1,0:T(8,128)(2,1)S(1)}, u32[]{:S(2)}, u32[]{:S(2)}) collective-permute-start(bf16[256,1152]{1,0:T(8,128)(2,1)S(1)} %pad_maximum_fusion.1), channel_id=1, source_target_pairs={{0,1},{1,0},{2,3},{3,2},{4,5},{5,4},{6,7},{7,6},{8,9},{9,8},{10,11... | collective-permute-start | bytes 1769480 | tf_op jit(solution)/shard_map/ppermute | solution.py:20
  106.2 0.0 collective-permute-done.5.refs_10_
  106.2 0.0 collective-permute-done.4.refs_9_
  106.2 2.9 %shard_map.69 = (f32[128,1152]{1,0:T(8,128)S(1)}, f32[128,1152]{1,0:T(8,128)S(1)}) custom-call(f32[1]{0:T(128)S(6)} %copy.9.refs_0_, f32[1]{0:T(128)S(6)} %copy.10.refs_1_, bf16[128,1152]{1,0:T(8,128)(2,1)S(1)} %copy-done, bf16[128,1152]{1,0:T(8,128)(2,1)S(1)} %copy-done.1, f32[128,1152]{1,0:T(8,128)S(1)} %get-tuple-element.13.refs_4_, ...), custom_call_target="tpu_custom_call" | custom-call | flops 603979776 | bytes 4128768 | tf_op jit(solution)/shard_map/pallas_call | solution.py:90
  109.1 0.0 collective-permute-done.8.refs_8_
  109.1 2.7 %shard_map.70 = (f32[128,1152]{1,0:T(8,128)}, f32[128,1152]{1,0:T(8,128)}) custom-call(f32[1]{0:T(128)S(6)} %copy.9.refs_0_, f32[1]{0:T(128)S(6)} %copy.10.refs_1_, bf16[128,1152]{1,0:T(8,128)(2,1)S(1)} %copy-done, bf16[128,1152]{1,0:T(8,128)(2,1)S(1)} %copy-done.1, f32[128,1152]{1,0:T(8,128)S(1)} %get-tuple-element.18.refs_4_, ...), custom_call_target="tpu_custom_call" | custom-call | flops 301989888 | bytes 2949120 | tf_op jit(solution)/shard_map/pallas_call | solution.py:90
  (9 shorter events, 0.2 us)
Async XLA Ops:
  0.6 23.6 %copy-start.1 = (bf16[128,1152]{1,0:T(8,128)(2,1)S(1)}, bf16[128,1152]{1,0:T(8,128)(2,1)}, u32[]{:S(2)}) copy-start(bf16[128,1152]{1,0:T(8,128)(2,1)} %refs_3_.5) | copy-start | bytes 884740
  0.6 1.1 copy-start
  0.6 35.7 %copy-start.2 = (s32[128]{0:T(128)S(1)}, s32[128]{0:T(128)}, u32[]{:S(2)}) copy-start(s32[128]{0:T(128)} %param.7) | copy-start | bytes 1540
  1.8 34.7 %collective-permute-start.3 = (bf16[256,1152]{1,0:T(8,128)(2,1)S(1)}, bf16[256,1152]{1,0:T(8,128)(2,1)S(1)}, u32[]{:S(2)}, u32[]{:S(2)}) collective-permute-start(bf16[256,1152]{1,0:T(8,128)(2,1)S(1)} %constant_dynamic-update-slice_fusion), channel_id=1, source_target_pairs={{0,1},{1,0},{2,3},{3,2},{4,5},{5,4},{6,7},{7,6},{8,9},{9,8},{10,11... | collective-permute-start | bytes 1769480 | tf_op jit(solution)/shard_map/ppermute | solution.py:20
  17.8 68.4 %collective-permute-start = (bf16[256,1152]{1,0:T(8,128)(2,1)S(1)}, bf16[256,1152]{1,0:T(8,128)(2,1)S(1)}, u32[]{:S(2)}, u32[]{:S(2)}) collective-permute-start(bf16[256,1152]{1,0:T(8,128)(2,1)S(1)} %constant_dynamic-update-slice_fusion), channel_id=1, source_target_pairs={{0,2},{1,3},{2,0},{3,1},{4,6},{5,7},{6,4},{7,5},{8,10},{9,11},{10,... | collective-permute-start | bytes 1769480 | tf_op jit(solution)/shard_map/ppermute | solution.py:20
  24.3 62.0 %collective-permute-start.1 = (bf16[128,1152]{1,0:T(8,128)(2,1)S(1)}, bf16[128,1152]{1,0:T(8,128)(2,1)S(1)}, u32[]{:S(2)}, u32[]{:S(2)}) collective-permute-start(bf16[128,1152]{1,0:T(8,128)(2,1)S(1)} %copy-done.1), channel_id=1, source_target_pairs={{0,4},{1,5},{2,6},{3,7},{4,8},{5,9},{6,10},{7,11},{8,12},{9,13},{1... | collective-permute-start | bytes 884744 | tf_op jit(solution)/shard_map/ppermute | solution.py:112
  27.4 58.8 %collective-permute-start.2 = (bf16[128,1152]{1,0:T(8,128)(2,1)S(1)}, bf16[128,1152]{1,0:T(8,128)(2,1)S(1)}, u32[]{:S(2)}, u32[]{:S(2)}) collective-permute-start(bf16[128,1152]{1,0:T(8,128)(2,1)S(1)} %copy-done), channel_id=1, source_target_pairs={{0,1022},{1,1023},{2,1020},{3,1021},{4,0},{5,1},{6,2},{7,3},{8,4},... | collective-permute-start | bytes 884744 | tf_op jit(solution)/shard_map/ppermute | solution.py:112
  86.3 15.7 %collective-permute-start.6 = (bf16[128,1152]{1,0:T(8,128)(2,1)S(1)}, bf16[128,1152]{1,0:T(8,128)(2,1)S(1)}, u32[]{:S(2)}, u32[]{:S(2)}) collective-permute-start(bf16[128,1152]{1,0:T(8,128)(2,1)S(1)} %get-tuple-element.21), channel_id=1, source_target_pairs={{0,4},{1,5},{2,6},{3,7},{4,8},{5,9},{6,10},{7,11},{8,12},{9,13},{1... | collective-permute-start | bytes 884744 | tf_op jit(solution)/shard_map/ppermute | solution.py:112
  88.2 14.4 %collective-permute-start.7 = (bf16[128,1152]{1,0:T(8,128)(2,1)S(1)}, bf16[128,1152]{1,0:T(8,128)(2,1)S(1)}, u32[]{:S(2)}, u32[]{:S(2)}) collective-permute-start(bf16[128,1152]{1,0:T(8,128)(2,1)S(1)} %get-tuple-element.20), channel_id=1, source_target_pairs={{0,1022},{1,1023},{2,1020},{3,1021},{4,0},{5,1},{6,2},{7,3},{8,4},... | collective-permute-start | bytes 884744 | tf_op jit(solution)/shard_map/ppermute | solution.py:112
  97.0 9.2 %collective-permute-start.4 = (bf16[256,1152]{1,0:T(8,128)(2,1)S(1)}, bf16[256,1152]{1,0:T(8,128)(2,1)S(1)}, u32[]{:S(2)}, u32[]{:S(2)}) collective-permute-start(bf16[256,1152]{1,0:T(8,128)(2,1)S(1)} %collective-permute-done.refs_8_), channel_id=1, source_target_pairs={{0,1},{1,0},{2,3},{3,2},{4,5},{5,4},{6,7},{7,6},{8,9},{9,8},{10,11... | collective-permute-start | bytes 1769480 | tf_op jit(solution)/shard_map/ppermute | solution.py:20
  100.0 6.2 %collective-permute-start.5 = (bf16[256,1152]{1,0:T(8,128)(2,1)S(1)}, bf16[256,1152]{1,0:T(8,128)(2,1)S(1)}, u32[]{:S(2)}, u32[]{:S(2)}) collective-permute-start(bf16[256,1152]{1,0:T(8,128)(2,1)S(1)} %pad_maximum_fusion), channel_id=1, source_target_pairs={{0,1},{1,0},{2,3},{3,2},{4,5},{5,4},{6,7},{7,6},{8,9},{9,8},{10,11... | collective-permute-start | bytes 1769480 | tf_op jit(solution)/shard_map/ppermute | solution.py:20
  102.7 6.5 %collective-permute-start.8 = (bf16[256,1152]{1,0:T(8,128)(2,1)S(1)}, bf16[256,1152]{1,0:T(8,128)(2,1)S(1)}, u32[]{:S(2)}, u32[]{:S(2)}) collective-permute-start(bf16[256,1152]{1,0:T(8,128)(2,1)S(1)} %pad_maximum_fusion.1), channel_id=1, source_target_pairs={{0,1},{1,0},{2,3},{3,2},{4,5},{5,4},{6,7},{7,6},{8,9},{9,8},{10,11... | collective-permute-start | bytes 1769480 | tf_op jit(solution)/shard_map/ppermute | solution.py:20

commit v3 on v0

v3 whole, which is shorter than its diff:
```python
import functools
import jax
import jax.numpy as jnp
from jax import lax
from jax.experimental import pallas as pl
from jax.experimental.pallas import tpu as pltpu
from jax.sharding import PartitionSpec as P

AXES = ("blk", "group")
norm_eps = 1e-06
RUN = 32
ROWS = 128
WEIGHT = 40


def moved_block(value, steps):
    blocks, groups = lax.axis_size("blk"), lax.axis_size("group")
    pairs = []
    for b in range(blocks):
        to = (b + steps) % blocks
        flip = 0 if b // RUN == to // RUN else groups // 2
        pairs += [(b * groups + g, to * groups + (g ^ flip)) for g in range(groups)]
    return lax.ppermute(value, AXES, pairs)


def moved_group(value, flip):
    blocks, groups = lax.axis_size("blk"), lax.axis_size("group")
    pairs = [(b * groups + g, b * groups + (g ^ flip)) for b in range(blocks) for g in range(groups)]
    return lax.ppermute(value, AXES, pairs)


def moved_half(value):
    return moved_group(value, lax.axis_size("group") // 2)


def moved_core(value):
    return moved_group(value, 1)


def unit_rows(values):
    wide = values.astype(jnp.float32)
    inverse = lax.rsqrt(jnp.sum(wide * wide, axis=-1, keepdims=True) + norm_eps)
    return (wide, inverse, (wide * inverse).astype(jnp.bfloat16))


def unit_backward(wide, inverse, upstream):
    inner = jnp.sum(wide * upstream, axis=-1, keepdims=True)
    return inverse * (upstream - inverse * inverse * wide * inner)


def dot_rows(a, b):
    return lax.dot_general(a, b, (((1,), (1,)), ((), ())), preferred_element_type=jnp.float32)


def dot_sum(coeff, unit):
    return jnp.dot(coeff.astype(jnp.bfloat16), unit, preferred_element_type=jnp.float32)


def add_met(total, scale, bias, unit, met_refs):
    rows = unit.shape[0]
    for ref, start in met_refs:
        met = unit_rows(ref[pl.ds(start, rows), :])[2]
        term = dot_sum(jax.nn.sigmoid(scale * dot_rows(unit, met) + bias), met)
        total = total + term
    return total


def first_kernel(texts, images, count, scale_ref, bias_ref, image_ref, text_ref, pos_ref, *refs):
    met, (image_out, text_out) = refs[:count], refs[count:]
    scale, bias = scale_ref[0], bias_ref[0]
    image_unit = unit_rows(image_ref[...])[2]
    text_unit = unit_rows(text_ref[...])[2]
    weights = jax.nn.sigmoid(scale * dot_rows(image_unit, text_unit) + bias)
    columns = lax.broadcasted_iota(jnp.int32, weights.shape, 1)
    weights = weights - (columns == pos_ref[...]).astype(jnp.float32)
    image_sum, text_sum = dot_sum(weights, text_unit), dot_sum(weights.T, image_unit)
    image_out[...] = add_met(image_sum, scale, bias, image_unit, [(met[k], s) for k, s in texts])
    text_out[...] = add_met(text_sum, scale, bias, text_unit, [(met[k], s) for k, s in images])


def next_kernel(jobs, count, scale_ref, bias_ref, *refs):
    met, refs = refs[:count], refs[count:]
    scale, bias = scale_ref[0], bias_ref[0]
    outs = refs[2 * len(jobs) :]
    for job, (places, final) in enumerate(jobs):
        wide, inverse, unit = unit_rows(refs[2 * job][...])
        total = add_met(refs[2 * job + 1][...], scale, bias, unit, [(met[k], s) for k, s in places])
        outs[job][...] = unit_backward(wide, inverse, scale * total) if final else total


SMEM = pl.BlockSpec(memory_space=pltpu.SMEM)
VMEM = pl.BlockSpec(memory_space=pltpu.VMEM)


def call(body, scalars, operands, outs, terms):
    width = operands[0].shape[1]
    out = jax.ShapeDtypeStruct((ROWS, width), jnp.float32)
    return pl.pallas_call(
        body,
        out_shape=(out,) * outs,
        in_specs=[SMEM] * 2 + [VMEM] * len(operands),
        out_specs=(VMEM,) * outs,
        compiler_params=pltpu.CompilerParams(vmem_limit_bytes=40 * 1024 * 1024),
        cost_estimate=pl.CostEstimate(
            flops=WEIGHT * 4 * ROWS * ROWS * width * terms,
            bytes_accessed=2 * ROWS * width * (terms + 4 * outs),
            transcendentals=ROWS * ROWS * terms,
        ),
    )(*scalars, *operands)


def first_terms(scalars, image, text, positives, met, texts, images):
    body = functools.partial(first_kernel, texts, images, len(met))
    return call(body, scalars, [image, text, positives[:, None], *met], 2, 2 + len(texts) + len(images))


def next_terms(scalars, met, *jobs):
    body = functools.partial(next_kernel, [job[2:] for job in jobs], len(met))
    own = [array for job in jobs for array in job[:2]]
    return call(body, scalars, [*met, *own], len(jobs), sum(len(job[2]) for job in jobs))


def local(image, text, positives, scale, bias):
    scalars = (scale, bias)
    far_text = moved_half(text)
    far_image = moved_half(image)
    last_text = moved_block(text, 1)
    next_image = moved_block(image, -1)
    twin = moved_core(jnp.concatenate([text, image]))
    sums = first_terms(scalars, image, text, positives, [twin], [(0, 0)], [(0, ROWS)])
    far_last_text = moved_block(far_text, 1)
    mid_twin = moved_core(jnp.concatenate([far_text, last_text, next_image]))
    far_next_image = moved_block(far_image, -1)
    image_sum, text_sum = next_terms(scalars, [far_text, last_text, next_image, mid_twin], (image, sums[0], [(0, 0), (1, 0), (3, 0), (3, ROWS)], False), (text, sums[1], [(2, 0), (3, 2 * ROWS)], False))
    late_twin = moved_core(jnp.concatenate([far_last_text, far_image]))
    image_grad, text_sum = next_terms(scalars, [far_last_text, far_image, late_twin], (image, image_sum, [(0, 0), (2, 0)], True), (text, text_sum, [(1, 0), (2, ROWS)], False))
    far_next_image, text_sum = lax.optimization_barrier((far_next_image, text_sum))
    last_twin = moved_core(far_next_image)
    (text_grad,) = next_terms(scalars, [far_next_image, last_twin], (text, text_sum, [(0, 0), (1, 0)], True))
    return (image_grad, text_grad)


def solution(mesh):
    in_specs = (P(AXES, None), P(AXES, None), P(AXES), P(), P())
    out_specs = (P(AXES, None), P(AXES, None))
    return jax.shard_map(local, mesh=mesh, in_specs=in_specs, out_specs=out_specs, check_vma=False)
```

time: 332 us -> 103 us (0.31)
  waiting for transfers between devices: 293 us -> 32.5 us
  starting transfers between devices: 9.65 us -> 59.2 us
  between operations: 15.1 us -> 2.11 us
  Pallas kernels: 0 us -> 7.45 us
  matrix products: 5.83 us -> 0 us
  other arithmetic: 6.47 us -> 1.21 us
    reduce_scatter x2 -> x0, waiting for transfers between devices: 188 us -> none  [local(): lax.psum_scatter(text_term, 'group', scatter_dimension=0, tiled=True)]
    all_gather x1 -> x0, waiting for transfers between devices: 69.7 us -> none  [local(): met_text = lax.all_gather(text_unit, 'group', axis=0, tiled=True)]
    ppermute x2 -> x10, starting transfers between devices: 9.53 us -> 59.2 us  [the longest x6 39.3 us: moved_group(): return lax.ppermute(value, AXES, pairs)]
    pallas_call x0 -> x4, Pallas kernels: none -> 7.45 us  [call(): pl.pallas_call(body, out_shape=(out,) * outs, in_specs=[SMEM] * 2 + [VMEM...]
    dot_general x6 -> x0, matrix products: 5.83 us -> none  [the longest x2 3.91 us: local(): lax.dot_general(coeff, image_unit, (((0,), (0,)), ((), ())), preferred_el...]
    ppermute x2 -> x10, waiting for transfers between devices: 35.7 us -> 32.5 us  [the longest x4 19.1 us: moved_block(): return lax.ppermute(value, AXES, pairs)]
  transfers between devices with their start and end apart: 5 -> 10, of which waited for: 4 -> 4; matrix products, arithmetic and copies ran while one was open for 1% -> 1% of each run, Pallas kernels for 0% -> 5%
where the time goes in v3:
time: 103 us
  starting transfers between devices  59.2 us (57%)
  waiting for transfers between devices  32.5 us (32%)
  Pallas kernels  7.45 us (7%)
  between operations  2.11 us (2%)
  other arithmetic  1.21 us (1%)
    ppermute x6, starting transfers between devices, moved_group(): return lax.ppermute(value, AXES, pairs)  39.3 us
    ppermute x4, starting transfers between devices, moved_block(): return lax.ppermute(value, AXES, pairs)  19.8 us
    ppermute x4, waiting for transfers between devices, moved_block(): return lax.ppermute(value, AXES, pairs)  19.1 us
    ppermute x6, waiting for transfers between devices, moved_group(): return lax.ppermute(value, AXES, pairs)  13.5 us
    pallas_call x4, Pallas kernels, call(): pl.pallas_call(body, out_shape=(out,) * outs, in_specs=[SMEM] * 2 + [VMEM...  7.45 us
  transfers between devices with their start and end apart: 10, of which 4 were waited for; matrix products, arithmetic and copies ran while one was open for 1% of the time, Pallas kernels for 5%

profile of v3, /device:TPU:1, one launch (start us, length us, event | category | flops | bytes accessed | tf_op | source)
XLA Modules:
  0.0 102.6 jit_solution(2438405732031491426)
XLA Ops:
  0.6 20.0 %collective-permute-start = (bf16[128,1152]{1,0:T(8,128)(2,1)}, bf16[128,1152]{1,0:T(8,128)(2,1)S(1)}, u32[]{:S(2)}, u32[]{:S(2)}) collective-permute-start(bf16[128,1152]{1,0:T(8,128)(2,1)} %refs_2_.1), channel_id=1, source_target_pairs={{0,2},{1,3},{2,0},{3,1},{4,6},{5,7},{6,4},{7,5},{8,10},{9,11},{10,... | collective-permute-start | bytes 884744 | tf_op jit(solution)/shard_map/ppermute | solution.py:29
  20.7 3.1 %collective-permute-start.4 = (bf16[128,1152]{1,0:T(8,128)(2,1)}, bf16[128,1152]{1,0:T(8,128)(2,1)S(1)}, u32[]{:S(2)}, u32[]{:S(2)}) collective-permute-start(bf16[128,1152]{1,0:T(8,128)(2,1)} %refs_2_.1), channel_id=1, source_target_pairs={{0,4},{1,5},{2,6},{3,7},{4,8},{5,9},{6,10},{7,11},{8,12},{9,13},{1... | collective-permute-start | bytes 884744 | tf_op jit(solution)/shard_map/ppermute | solution.py:23
  23.8 7.6 %collective-permute-start.5 = (bf16[128,1152]{1,0:T(8,128)(2,1)}, bf16[128,1152]{1,0:T(8,128)(2,1)S(1)}, u32[]{:S(2)}, u32[]{:S(2)}) collective-permute-start(bf16[128,1152]{1,0:T(8,128)(2,1)} %refs_3_.1), channel_id=1, source_target_pairs={{0,1022},{1,1023},{2,1020},{3,1021},{4,0},{5,1},{6,2},{7,3},{8,4},... | collective-permute-start | bytes 884744 | tf_op jit(solution)/shard_map/ppermute | solution.py:23
  31.4 1.1 %pad_maximum_fusion.2 = bf16[256,1152]{1,0:T(8,128)(2,1)S(1)} fusion(bf16[128,1152]{1,0:T(8,128)(2,1)} %refs_3_.1, bf16[128,1152]{1,0:T(8,128)(2,1)} %refs_2_.1), kind=kLoop, calls=%fused_computation.2 | loop fusion | flops 1179648 | bytes 1179648 | tf_op jit(solution)/shard_map/concatenate | solution.py:129
  32.5 3.4 %collective-permute-start.7 = (bf16[256,1152]{1,0:T(8,128)(2,1)S(1)}, bf16[256,1152]{1,0:T(8,128)(2,1)S(1)}, u32[]{:S(2)}, u32[]{:S(2)}) collective-permute-start(bf16[256,1152]{1,0:T(8,128)(2,1)S(1)} %pad_maximum_fusion.2), channel_id=1, source_target_pairs={{0,1},{1,0},{2,3},{3,2},{4,5},{5,4},{6,7},{7,6},{8,9},{9,8},{10,11... | collective-permute-start | bytes 1769480 | tf_op jit(solution)/shard_map/ppermute | solution.py:29
  36.0 8.9 %collective-permute-start.2 = (bf16[128,1152]{1,0:T(8,128)(2,1)S(1)}, bf16[128,1152]{1,0:T(8,128)(2,1)S(1)}, u32[]{:S(2)}, u32[]{:S(2)}) collective-permute-start(bf16[128,1152]{1,0:T(8,128)(2,1)S(1)} %copy-done), channel_id=1, source_target_pairs={{0,2},{1,3},{2,0},{3,1},{4,6},{5,7},{6,4},{7,5},{8,10},{9,11},{10,... | collective-permute-start | bytes 884744 | tf_op jit(solution)/shard_map/ppermute | solution.py:29
  44.9 0.0 collective-permute-done.refs_0_
  44.9 1.9 %collective-permute-start.1 = (bf16[128,1152]{1,0:T(8,128)(2,1)S(1)}, bf16[128,1152]{1,0:T(8,128)(2,1)S(1)}, u32[]{:S(2)}, u32[]{:S(2)}) collective-permute-start(bf16[128,1152]{1,0:T(8,128)(2,1)S(1)} %collective-permute-done.refs_0_), channel_id=1, source_target_pairs={{0,4},{1,5},{2,6},{3,7},{4,8},{5,9},{6,10},{7,11},{8,12},{9,13},{1... | collective-permute-start | bytes 884744 | tf_op jit(solution)/shard_map/ppermute | solution.py:23
  48.1 0.1 copy.7.pos_ref
  48.2 12.6 %collective-permute-done.4.refs_1_ = bf16[128,1152]{1,0:T(8,128)(2,1)S(1)} collective-permute-done((bf16[128,1152]{1,0:T(8,128)(2,1)}, bf16[128,1152]{1,0:T(8,128)(2,1)S(1)}, u32[]{:S(2)}, u32[]{:S(2)}) %collective-permute-start.4) | collective-permute-done | bytes 294944 | tf_op jit(solution)/shard_map/ppermute | solution.py:23
  60.9 0.1 pad_maximum_fusion
  60.9 0.0 copy-start.1
  61.0 2.6 %collective-permute-start.6 = (bf16[384,1152]{1,0:T(8,128)(2,1)S(1)}, bf16[384,1152]{1,0:T(8,128)(2,1)S(1)}, u32[]{:S(2)}, u32[]{:S(2)}) collective-permute-start(bf16[384,1152]{1,0:T(8,128)(2,1)S(1)} %pad_maximum_fusion), channel_id=1, source_target_pairs={{0,1},{1,0},{2,3},{3,2},{4,5},{5,4},{6,7},{7,6},{8,9},{9,8},{10,11... | collective-permute-start | bytes 2654216 | tf_op jit(solution)/shard_map/ppermute | solution.py:29
  63.6 11.9 %collective-permute-done.2.refs_1_ = bf16[128,1152]{1,0:T(8,128)(2,1)S(1)} collective-permute-done((bf16[128,1152]{1,0:T(8,128)(2,1)S(1)}, bf16[128,1152]{1,0:T(8,128)(2,1)S(1)}, u32[]{:S(2)}, u32[]{:S(2)}) %collective-permute-start.2) | collective-permute-done | bytes 294944 | tf_op jit(solution)/shard_map/ppermute | solution.py:29
  75.5 7.2 %collective-permute-start.8 = (bf16[128,1152]{1,0:T(8,128)(2,1)S(1)}, bf16[128,1152]{1,0:T(8,128)(2,1)S(1)}, u32[]{:S(2)}, u32[]{:S(2)}) collective-permute-start(bf16[128,1152]{1,0:T(8,128)(2,1)S(1)} %collective-permute-done.2.refs_1_), channel_id=1, source_target_pairs={{0,1022},{1,1023},{2,1020},{3,1021},{4,0},{5,1},{6,2},{7,3},{8,4},... | collective-permute-start | bytes 884744 | tf_op jit(solution)/shard_map/ppermute | solution.py:23
  82.7 6.4 %collective-permute-done.1.refs_0_ = bf16[128,1152]{1,0:T(8,128)(2,1)S(1)} collective-permute-done((bf16[128,1152]{1,0:T(8,128)(2,1)S(1)}, bf16[128,1152]{1,0:T(8,128)(2,1)S(1)}, u32[]{:S(2)}, u32[]{:S(2)}) %collective-permute-start.1) | collective-permute-done | bytes 294944 | tf_op jit(solution)/shard_map/ppermute | solution.py:23
  89.2 2.4 %collective-permute-start.3 = (bf16[256,1152]{1,0:T(8,128)(2,1)S(1)}, bf16[256,1152]{1,0:T(8,128)(2,1)S(1)}, u32[]{:S(2)}, u32[]{:S(2)}) collective-permute-start(bf16[256,1152]{1,0:T(8,128)(2,1)S(1)} %pad_maximum_fusion.1), channel_id=1, source_target_pairs={{0,1},{1,0},{2,3},{3,2},{4,5},{5,4},{6,7},{7,6},{8,9},{9,8},{10,11... | collective-permute-start | bytes 1769480 | tf_op jit(solution)/shard_map/ppermute | solution.py:29
  91.6 0.0 collective-permute-done.7.refs_0_
  91.7 1.3 %shard_map.68 = (f32[128,1152]{1,0:T(8,128)S(1)}, f32[128,1152]{1,0:T(8,128)S(1)}) custom-call(f32[1]{0:T(128)S(6)} %copy.8.scale_ref, f32[1]{0:T(128)S(6)} %copy.9.bias_ref, bf16[128,1152]{1,0:T(8,128)(2,1)S(1)} %copy-done, bf16[128,1152]{1,0:T(8,128)(2,1)S(1)} %copy-done.1, s32[128,1]{1,0:T(8,128)S(1)} %copy.7.pos_ref, ...), custom_call_target="tpu_custom_call" | custom-call | flops 12079595520 | bytes 3538944 | tf_op jit(solution)/shard_map/pallas_call | solution.py:98
  92.9 2.2 %shard_map.69 = (f32[128,1152]{1,0:T(8,128)S(1)}, f32[128,1152]{1,0:T(8,128)S(1)}) custom-call(f32[1]{0:T(128)S(6)} %copy.8.scale_ref, f32[1]{0:T(128)S(6)} %copy.9.bias_ref, bf16[128,1152]{1,0:T(8,128)(2,1)S(1)} %collective-permute-done.refs_0_, bf16[128,1152]{1,0:T(8,128)(2,1)S(1)} %collective-permute-done.4.refs_1_, ...), custom_call_target="tpu_custom_call" | custom-call | flops 18119393280 | bytes 4128768 | tf_op jit(solution)/shard_map/pallas_call | solution.py:98
  95.2 2.0 %shard_map.70 = (f32[128,1152]{1,0:T(8,128)}, f32[128,1152]{1,0:T(8,128)S(1)}) custom-call(f32[1]{0:T(128)S(6)} %copy.8.scale_ref, f32[1]{0:T(128)S(6)} %copy.9.bias_ref, bf16[128,1152]{1,0:T(8,128)(2,1)S(1)} %collective-permute-done.1.refs_0_, bf16[128,1152]{1,0:T(8,128)(2,1)S(1)} %collective-permute-done.2.refs_1_, ...), custom_call_target="tpu_custom_call" | custom-call | flops 12079595520 | bytes 3538944 | tf_op jit(solution)/shard_map/pallas_call | solution.py:98
  97.2 1.9 %collective-permute-start.9 = (bf16[128,1152]{1,0:T(8,128)(2,1)S(1)}, bf16[128,1152]{1,0:T(8,128)(2,1)S(1)}, u32[]{:S(2)}, u32[]{:S(2)}) collective-permute-start(bf16[128,1152]{1,0:T(8,128)(2,1)S(1)} %collective-permute-done.8.refs_0_), channel_id=1, source_target_pairs={{0,1},{1,0},{2,3},{3,2},{4,5},{5,4},{6,7},{7,6},{8,9},{9,8},{10,11... | collective-permute-start | bytes 884744 | tf_op jit(solution)/shard_map/ppermute | solution.py:29
  99.1 1.5 %collective-permute-done.9.refs_1_ = bf16[128,1152]{1,0:T(8,128)(2,1)S(1)} collective-permute-done((bf16[128,1152]{1,0:T(8,128)(2,1)S(1)}, bf16[128,1152]{1,0:T(8,128)(2,1)S(1)}, u32[]{:S(2)}, u32[]{:S(2)}) %collective-permute-start.9) | collective-permute-done | bytes 294944 | tf_op jit(solution)/shard_map/ppermute | solution.py:29
  100.7 2.0 %shard_map.71 = f32[128,1152]{1,0:T(8,128)} custom-call(f32[1]{0:T(128)S(6)} %copy.8.scale_ref, f32[1]{0:T(128)S(6)} %copy.9.bias_ref, bf16[128,1152]{1,0:T(8,128)(2,1)S(1)} %collective-permute-done.8.refs_0_, bf16[128,1152]{1,0:T(8,128)(2,1)S(1)} %collective-permute-done.9.refs_1_, bf16[128,1152]{1,0:T(8,128)(2,1)S(1)} %copy-done.1, ...), custom_call_target="tpu_custom_call" | custom-call | flops 6039797760 | bytes 1769472 | tf_op jit(solution)/shard_map/pallas_call | solution.py:98
  (10 shorter events, 0.1 us)
Async XLA Ops:
  0.6 35.3 %copy-start = (bf16[128,1152]{1,0:T(8,128)(2,1)S(1)}, bf16[128,1152]{1,0:T(8,128)(2,1)}, u32[]{:S(2)}) copy-start(bf16[128,1152]{1,0:T(8,128)(2,1)} %refs_3_.1) | copy-start | bytes 884740
  0.6 47.5 %copy-start.2 = (s32[128]{0:T(128)S(1)}, s32[128]{0:T(128)}, u32[]{:S(2)}) copy-start(s32[128]{0:T(128)} %param.7) | copy-start | bytes 1540
  0.6 44.2 %collective-permute-start = (bf16[128,1152]{1,0:T(8,128)(2,1)}, bf16[128,1152]{1,0:T(8,128)(2,1)S(1)}, u32[]{:S(2)}, u32[]{:S(2)}) collective-permute-start(bf16[128,1152]{1,0:T(8,128)(2,1)} %refs_2_.1), channel_id=1, source_target_pairs={{0,2},{1,3},{2,0},{3,1},{4,6},{5,7},{6,4},{7,5},{8,10},{9,11},{10,... | collective-permute-start | bytes 884744 | tf_op jit(solution)/shard_map/ppermute | solution.py:29
  20.7 40.2 %collective-permute-start.4 = (bf16[128,1152]{1,0:T(8,128)(2,1)}, bf16[128,1152]{1,0:T(8,128)(2,1)S(1)}, u32[]{:S(2)}, u32[]{:S(2)}) collective-permute-start(bf16[128,1152]{1,0:T(8,128)(2,1)} %refs_2_.1), channel_id=1, source_target_pairs={{0,4},{1,5},{2,6},{3,7},{4,8},{5,9},{6,10},{7,11},{8,12},{9,13},{1... | collective-permute-start | bytes 884744 | tf_op jit(solution)/shard_map/ppermute | solution.py:23
  23.8 37.0 %collective-permute-start.5 = (bf16[128,1152]{1,0:T(8,128)(2,1)}, bf16[128,1152]{1,0:T(8,128)(2,1)S(1)}, u32[]{:S(2)}, u32[]{:S(2)}) collective-permute-start(bf16[128,1152]{1,0:T(8,128)(2,1)} %refs_3_.1), channel_id=1, source_target_pairs={{0,1022},{1,1023},{2,1020},{3,1021},{4,0},{5,1},{6,2},{7,3},{8,4},... | collective-permute-start | bytes 884744 | tf_op jit(solution)/shard_map/ppermute | solution.py:23
  32.5 59.1 %collective-permute-start.7 = (bf16[256,1152]{1,0:T(8,128)(2,1)S(1)}, bf16[256,1152]{1,0:T(8,128)(2,1)S(1)}, u32[]{:S(2)}, u32[]{:S(2)}) collective-permute-start(bf16[256,1152]{1,0:T(8,128)(2,1)S(1)} %pad_maximum_fusion.2), channel_id=1, source_target_pairs={{0,1},{1,0},{2,3},{3,2},{4,5},{5,4},{6,7},{7,6},{8,9},{9,8},{10,11... | collective-permute-start | bytes 1769480 | tf_op jit(solution)/shard_map/ppermute | solution.py:29
  36.0 39.5 %collective-permute-start.2 = (bf16[128,1152]{1,0:T(8,128)(2,1)S(1)}, bf16[128,1152]{1,0:T(8,128)(2,1)S(1)}, u32[]{:S(2)}, u32[]{:S(2)}) collective-permute-start(bf16[128,1152]{1,0:T(8,128)(2,1)S(1)} %copy-done), channel_id=1, source_target_pairs={{0,2},{1,3},{2,0},{3,1},{4,6},{5,7},{6,4},{7,5},{8,10},{9,11},{10,... | collective-permute-start | bytes 884744 | tf_op jit(solution)/shard_map/ppermute | solution.py:29
  44.9 44.3 %collective-permute-start.1 = (bf16[128,1152]{1,0:T(8,128)(2,1)S(1)}, bf16[128,1152]{1,0:T(8,128)(2,1)S(1)}, u32[]{:S(2)}, u32[]{:S(2)}) collective-permute-start(bf16[128,1152]{1,0:T(8,128)(2,1)S(1)} %collective-permute-done.refs_0_), channel_id=1, source_target_pairs={{0,4},{1,5},{2,6},{3,7},{4,8},{5,9},{6,10},{7,11},{8,12},{9,13},{1... | collective-permute-start | bytes 884744 | tf_op jit(solution)/shard_map/ppermute | solution.py:23
  60.9 30.7 %copy-start.1 = (bf16[128,1152]{1,0:T(8,128)(2,1)S(1)}, bf16[128,1152]{1,0:T(8,128)(2,1)}, u32[]{:S(2)}) copy-start(bf16[128,1152]{1,0:T(8,128)(2,1)} %refs_2_.1) | copy-start | bytes 884740
  61.0 32.0 %collective-permute-start.6 = (bf16[384,1152]{1,0:T(8,128)(2,1)S(1)}, bf16[384,1152]{1,0:T(8,128)(2,1)S(1)}, u32[]{:S(2)}, u32[]{:S(2)}) collective-permute-start(bf16[384,1152]{1,0:T(8,128)(2,1)S(1)} %pad_maximum_fusion), channel_id=1, source_target_pairs={{0,1},{1,0},{2,3},{3,2},{4,5},{5,4},{6,7},{7,6},{8,9},{9,8},{10,11... | collective-permute-start | bytes 2654216 | tf_op jit(solution)/shard_map/ppermute | solution.py:29
  75.5 21.7 %collective-permute-start.8 = (bf16[128,1152]{1,0:T(8,128)(2,1)S(1)}, bf16[128,1152]{1,0:T(8,128)(2,1)S(1)}, u32[]{:S(2)}, u32[]{:S(2)}) collective-permute-start(bf16[128,1152]{1,0:T(8,128)(2,1)S(1)} %collective-permute-done.2.refs_1_), channel_id=1, source_target_pairs={{0,1022},{1,1023},{2,1020},{3,1021},{4,0},{5,1},{6,2},{7,3},{8,4},... | collective-permute-start | bytes 884744 | tf_op jit(solution)/shard_map/ppermute | solution.py:23
  89.2 5.9 %collective-permute-start.3 = (bf16[256,1152]{1,0:T(8,128)(2,1)S(1)}, bf16[256,1152]{1,0:T(8,128)(2,1)S(1)}, u32[]{:S(2)}, u32[]{:S(2)}) collective-permute-start(bf16[256,1152]{1,0:T(8,128)(2,1)S(1)} %pad_maximum_fusion.1), channel_id=1, source_target_pairs={{0,1},{1,0},{2,3},{3,2},{4,5},{5,4},{6,7},{7,6},{8,9},{9,8},{10,11... | collective-permute-start | bytes 1769480 | tf_op jit(solution)/shard_map/ppermute | solution.py:29
  97.2 3.5 %collective-permute-start.9 = (bf16[128,1152]{1,0:T(8,128)(2,1)S(1)}, bf16[128,1152]{1,0:T(8,128)(2,1)S(1)}, u32[]{:S(2)}, u32[]{:S(2)}) collective-permute-start(bf16[128,1152]{1,0:T(8,128)(2,1)S(1)} %collective-permute-done.8.refs_0_), channel_id=1, source_target_pairs={{0,1},{1,0},{2,3},{3,2},{4,5},{5,4},{6,7},{7,6},{8,9},{9,8},{10,11... | collective-permute-start | bytes 884744 | tf_op jit(solution)/shard_map/ppermute | solution.py:29

commit v4 on v3

--- a/solution.py
+++ b/solution.py
@@ -10,7 +10,7 @@
 norm_eps = 1e-06
 RUN = 32
 ROWS = 128
-WEIGHT = 40
+WEIGHTS = (40, 40, 40, 40)
 
 
 def moved_block(value, steps):
@@ -58,11 +58,8 @@
 
 def add_met(total, scale, bias, unit, met_refs):
     rows = unit.shape[0]
-    for ref, start in met_refs:
-        met = unit_rows(ref[pl.ds(start, rows), :])[2]
-        term = dot_sum(jax.nn.sigmoid(scale * dot_rows(unit, met) + bias), met)
-        total = total + term
-    return total
+    met = jnp.concatenate([unit_rows(ref[pl.ds(start, rows), :])[2] for ref, start in met_refs])
+    return total + dot_sum(jax.nn.sigmoid(scale * dot_rows(unit, met) + bias), met)
 
 
 def first_kernel(texts, images, count, scale_ref, bias_ref, image_ref, text_ref, pos_ref, *refs):
@@ -92,7 +89,7 @@
 VMEM = pl.BlockSpec(memory_space=pltpu.VMEM)
 
 
-def call(body, scalars, operands, outs, terms):
+def call(turn, body, scalars, operands, outs, terms):
     width = operands[0].shape[1]
     out = jax.ShapeDtypeStruct((ROWS, width), jnp.float32)
     return pl.pallas_call(
@@ -102,7 +99,7 @@
         out_specs=(VMEM,) * outs,
         compiler_params=pltpu.CompilerParams(vmem_limit_bytes=40 * 1024 * 1024),
         cost_estimate=pl.CostEstimate(
-            flops=WEIGHT * 4 * ROWS * ROWS * width * terms,
+            flops=WEIGHTS[turn] * 4 * ROWS * ROWS * width * terms,
             bytes_accessed=2 * ROWS * width * (terms + 4 * outs),
             transcendentals=ROWS * ROWS * terms,
         ),
@@ -111,13 +108,13 @@
 
 def first_terms(scalars, image, text, positives, met, texts, images):
     body = functools.partial(first_kernel, texts, images, len(met))
-    return call(body, scalars, [image, text, positives[:, None], *met], 2, 2 + len(texts) + len(images))
+    return call(0, body, scalars, [image, text, positives[:, None], *met], 2, 2 + len(texts) + len(images))
 
 
-def next_terms(scalars, met, *jobs):
+def next_terms(turn, scalars, met, *jobs):
     body = functools.partial(next_kernel, [job[2:] for job in jobs], len(met))
     own = [array for job in jobs for array in job[:2]]
-    return call(body, scalars, [*met, *own], len(jobs), sum(len(job[2]) for job in jobs))
+    return call(turn, body, scalars, [*met, *own], len(jobs), sum(len(job[2]) for job in jobs))
 
 
 def local(image, text, positives, scale, bias):
@@ -130,14 +127,25 @@
     sums = first_terms(scalars, image, text, positives, [twin], [(0, 0)], [(0, ROWS)])
     far_last_text = moved_block(far_text, 1)
     mid_twin = moved_core(jnp.concatenate([far_text, last_text, next_image]))
+    sums = next_terms(
+        1,
+        scalars,
+        [far_text, last_text, next_image, mid_twin],
+        (image, sums[0], [(0, 0), (1, 0), (3, 0), (3, ROWS)], False),
+        (text, sums[1], [(2, 0), (3, 2 * ROWS)], False),
+    )
     far_next_image = moved_block(far_image, -1)
-    image_sum, text_sum = next_terms(scalars, [far_text, last_text, next_image, mid_twin], (image, sums[0], [(0, 0), (1, 0), (3, 0), (3, ROWS)], False), (text, sums[1], [(2, 0), (3, 2 * ROWS)], False))
-    late_twin = moved_core(jnp.concatenate([far_last_text, far_image]))
-    image_grad, text_sum = next_terms(scalars, [far_last_text, far_image, late_twin], (image, image_sum, [(0, 0), (2, 0)], True), (text, text_sum, [(1, 0), (2, ROWS)], False))
-    far_next_image, text_sum = lax.optimization_barrier((far_next_image, text_sum))
-    last_twin = moved_core(far_next_image)
-    (text_grad,) = next_terms(scalars, [far_next_image, last_twin], (text, text_sum, [(0, 0), (1, 0)], True))
-    return (image_grad, text_grad)
+    image_sum, text_sum = sums
+    image_twin = moved_core(far_image)
+    (text_sum,) = next_terms(2, scalars, [far_image, image_twin], (text, text_sum, [(0, 0), (1, 0)], False))
+    last_twin = moved_core(jnp.concatenate([far_last_text, far_next_image]))
+    return next_terms(
+        3,
+        scalars,
+        [far_last_text, far_next_image, last_twin],
+        (image, image_sum, [(0, 0), (2, 0)], True),
+        (text, text_sum, [(1, 0), (2, ROWS)], True),
+    )
 
 
 def solution(mesh):

time: 103 us -> 98.9 us (0.960)
  waiting for transfers between devices: 32.5 us -> 17.4 us
  starting transfers between devices: 59.2 us -> 71.2 us
  Pallas kernels: 7.45 us -> 6.37 us
    ppermute x4, starting transfers between devices: 19.8 us -> 36.9 us  [moved_block(): return lax.ppermute(value, AXES, pairs)]
    ppermute x6, waiting for transfers between devices: 13.5 us -> 0.02 us  [moved_group(): return lax.ppermute(value, AXES, pairs)]
    ppermute x6, starting transfers between devices: 39.3 us -> 34.3 us  [moved_group(): return lax.ppermute(value, AXES, pairs)]
    ppermute x4, waiting for transfers between devices: 19.1 us -> 17.4 us  [moved_block(): return lax.ppermute(value, AXES, pairs)]
    pallas_call x4, Pallas kernels: 7.45 us -> 6.37 us  [call(): pl.pallas_call(body, out_shape=(out,) * outs, in_specs=[SMEM] * 2 + [VMEM...]
  transfers between devices with their start and end apart: 10 -> 10, of which waited for: 4 -> 1; matrix products, arithmetic and copies ran while one was open for 1% -> 1% of each run, Pallas kernels for 5% -> 4%
where the time goes in v4:
time: 98.9 us; the launch traced here: 98.5 us
  starting transfers between devices  71.2 us (72%)
  waiting for transfers between devices  17.4 us (18%)
  Pallas kernels  6.37 us (6%)
  between operations  2.15 us (2%)
  other arithmetic  1.21 us (1%)
    ppermute x4, starting transfers between devices, moved_block(): return lax.ppermute(value, AXES, pairs)  36.9 us
    ppermute x6, starting transfers between devices, moved_group(): return lax.ppermute(value, AXES, pairs)  34.3 us
    ppermute x4, waiting for transfers between devices, moved_block(): return lax.ppermute(value, AXES, pairs)  17.4 us
    pallas_call x4, Pallas kernels, call(): pl.pallas_call(body, out_shape=(out,) * outs, in_specs=[SMEM] * 2 + [VMEM...  6.37 us
  transfers between devices with their start and end apart: 10, of which 1 were waited for; matrix products, arithmetic and copies ran while one was open for 1% of the time, Pallas kernels for 4%

profile of v4, /device:TPU:1, one launch (start us, length us, event | category | flops | bytes accessed | tf_op | source)
XLA Modules:
  0.0 98.5 jit_solution(5585588270279312741)
XLA Ops:
  0.6 19.9 %collective-permute-start = (bf16[128,1152]{1,0:T(8,128)(2,1)}, bf16[128,1152]{1,0:T(8,128)(2,1)S(1)}, u32[]{:S(2)}, u32[]{:S(2)}) collective-permute-start(bf16[128,1152]{1,0:T(8,128)(2,1)} %refs_5_.1), channel_id=1, source_target_pairs={{0,2},{1,3},{2,0},{3,1},{4,6},{5,7},{6,4},{7,5},{8,10},{9,11},{10,... | collective-permute-start | bytes 884744 | tf_op jit(solution)/shard_map/ppermute | solution.py:29
  20.6 1.9 %collective-permute-start.2 = (bf16[128,1152]{1,0:T(8,128)(2,1)}, bf16[128,1152]{1,0:T(8,128)(2,1)S(1)}, u32[]{:S(2)}, u32[]{:S(2)}) collective-permute-start(bf16[128,1152]{1,0:T(8,128)(2,1)} %refs_3_.1), channel_id=1, source_target_pairs={{0,2},{1,3},{2,0},{3,1},{4,6},{5,7},{6,4},{7,5},{8,10},{9,11},{10,... | collective-permute-start | bytes 884744 | tf_op jit(solution)/shard_map/ppermute | solution.py:29
  22.5 3.1 %collective-permute-start.5 = (bf16[128,1152]{1,0:T(8,128)(2,1)}, bf16[128,1152]{1,0:T(8,128)(2,1)S(1)}, u32[]{:S(2)}, u32[]{:S(2)}) collective-permute-start(bf16[128,1152]{1,0:T(8,128)(2,1)} %refs_5_.1), channel_id=1, source_target_pairs={{0,4},{1,5},{2,6},{3,7},{4,8},{5,9},{6,10},{7,11},{8,12},{9,13},{1... | collective-permute-start | bytes 884744 | tf_op jit(solution)/shard_map/ppermute | solution.py:23
  25.6 14.8 %collective-permute-start.6 = (bf16[128,1152]{1,0:T(8,128)(2,1)}, bf16[128,1152]{1,0:T(8,128)(2,1)S(1)}, u32[]{:S(2)}, u32[]{:S(2)}) collective-permute-start(bf16[128,1152]{1,0:T(8,128)(2,1)} %refs_3_.1), channel_id=1, source_target_pairs={{0,1022},{1,1023},{2,1020},{3,1021},{4,0},{5,1},{6,2},{7,3},{8,4},... | collective-permute-start | bytes 884744 | tf_op jit(solution)/shard_map/ppermute | solution.py:23
  40.5 1.1 %pad_maximum_fusion.2 = bf16[256,1152]{1,0:T(8,128)(2,1)S(1)} fusion(bf16[128,1152]{1,0:T(8,128)(2,1)} %refs_3_.1, bf16[128,1152]{1,0:T(8,128)(2,1)} %refs_5_.1), kind=kLoop, calls=%fused_computation.2 | loop fusion | flops 1179648 | bytes 1179648 | tf_op jit(solution)/shard_map/concatenate | solution.py:126
  41.6 3.4 %collective-permute-start.8 = (bf16[256,1152]{1,0:T(8,128)(2,1)S(1)}, bf16[256,1152]{1,0:T(8,128)(2,1)S(1)}, u32[]{:S(2)}, u32[]{:S(2)}) collective-permute-start(bf16[256,1152]{1,0:T(8,128)(2,1)S(1)} %pad_maximum_fusion.2), channel_id=1, source_target_pairs={{0,1},{1,0},{2,3},{3,2},{4,5},{5,4},{6,7},{7,6},{8,9},{9,8},{10,11... | collective-permute-start | bytes 1769480 | tf_op jit(solution)/shard_map/ppermute | solution.py:29
  45.0 0.0 collective-permute-done.refs_0_
  45.0 1.9 %collective-permute-start.1 = (bf16[128,1152]{1,0:T(8,128)(2,1)S(1)}, bf16[128,1152]{1,0:T(8,128)(2,1)S(1)}, u32[]{:S(2)}, u32[]{:S(2)}) collective-permute-start(bf16[128,1152]{1,0:T(8,128)(2,1)S(1)} %collective-permute-done.refs_0_), channel_id=1, source_target_pairs={{0,4},{1,5},{2,6},{3,7},{4,8},{5,9},{6,10},{7,11},{8,12},{9,13},{1... | collective-permute-start | bytes 884744 | tf_op jit(solution)/shard_map/ppermute | solution.py:23
  46.9 0.0 collective-permute-done.2.refs_0_
  47.0 17.1 %collective-permute-start.3 = (bf16[128,1152]{1,0:T(8,128)(2,1)S(1)}, bf16[128,1152]{1,0:T(8,128)(2,1)S(1)}, u32[]{:S(2)}, u32[]{:S(2)}) collective-permute-start(bf16[128,1152]{1,0:T(8,128)(2,1)S(1)} %collective-permute-done.2.refs_0_), channel_id=1, source_target_pairs={{0,1022},{1,1023},{2,1020},{3,1021},{4,0},{5,1},{6,2},{7,3},{8,4},... | collective-permute-start | bytes 884744 | tf_op jit(solution)/shard_map/ppermute | solution.py:23
  65.3 0.1 copy.7.pos_ref
  65.4 17.4 %collective-permute-done.5.refs_1_ = bf16[128,1152]{1,0:T(8,128)(2,1)S(1)} collective-permute-done((bf16[128,1152]{1,0:T(8,128)(2,1)}, bf16[128,1152]{1,0:T(8,128)(2,1)S(1)}, u32[]{:S(2)}, u32[]{:S(2)}) %collective-permute-start.5) | collective-permute-done | bytes 294944 | tf_op jit(solution)/shard_map/ppermute | solution.py:23
  82.8 0.0 collective-permute-done.6.refs_2_
  82.8 0.1 pad_maximum_fusion
  82.9 0.0 copy-start
  82.9 0.0 copy-start.1
  82.9 4.7 %collective-permute-start.7 = (bf16[384,1152]{1,0:T(8,128)(2,1)S(1)}, bf16[384,1152]{1,0:T(8,128)(2,1)S(1)}, u32[]{:S(2)}, u32[]{:S(2)}) collective-permute-start(bf16[384,1152]{1,0:T(8,128)(2,1)S(1)} %pad_maximum_fusion), channel_id=1, source_target_pairs={{0,1},{1,0},{2,3},{3,2},{4,5},{5,4},{6,7},{7,6},{8,9},{9,8},{10,11... | collective-permute-start | bytes 2654216 | tf_op jit(solution)/shard_map/ppermute | solution.py:29
  87.6 1.9 %collective-permute-start.9 = (bf16[128,1152]{1,0:T(8,128)(2,1)S(1)}, bf16[128,1152]{1,0:T(8,128)(2,1)S(1)}, u32[]{:S(2)}, u32[]{:S(2)}) collective-permute-start(bf16[128,1152]{1,0:T(8,128)(2,1)S(1)} %collective-permute-done.2.refs_0_), channel_id=1, source_target_pairs={{0,1},{1,0},{2,3},{3,2},{4,5},{5,4},{6,7},{7,6},{8,9},{9,8},{10,11... | collective-permute-start | bytes 884744 | tf_op jit(solution)/shard_map/ppermute | solution.py:29
  89.6 2.4 %collective-permute-start.4 = (bf16[256,1152]{1,0:T(8,128)(2,1)S(1)}, bf16[256,1152]{1,0:T(8,128)(2,1)S(1)}, u32[]{:S(2)}, u32[]{:S(2)}) collective-permute-start(bf16[256,1152]{1,0:T(8,128)(2,1)S(1)} %pad_maximum_fusion.1), channel_id=1, source_target_pairs={{0,1},{1,0},{2,3},{3,2},{4,5},{5,4},{6,7},{7,6},{8,9},{9,8},{10,11... | collective-permute-start | bytes 1769480 | tf_op jit(solution)/shard_map/ppermute | solution.py:29
  92.1 1.3 %shard_map.68 = (f32[128,1152]{1,0:T(8,128)S(1)}, f32[128,1152]{1,0:T(8,128)S(1)}) custom-call(f32[1]{0:T(128)S(6)} %copy.8.scale_ref, f32[1]{0:T(128)S(6)} %copy.9.bias_ref, bf16[128,1152]{1,0:T(8,128)(2,1)S(1)} %copy-done.1, bf16[128,1152]{1,0:T(8,128)(2,1)S(1)} %copy-done, s32[128,1]{1,0:T(8,128)S(1)} %copy.7.pos_ref, ...), custom_call_target="tpu_custom_call" | custom-call | flops 12079595520 | bytes 3538944 | tf_op jit(solution)/shard_map/pallas_call | solution.py:95
  93.4 0.0 collective-permute-done.7.refs_3_
  93.4 1.7 %shard_map.69 = (f32[128,1152]{1,0:T(8,128)S(1)}, f32[128,1152]{1,0:T(8,128)S(1)}) custom-call(f32[1]{0:T(128)S(6)} %copy.8.scale_ref, f32[1]{0:T(128)S(6)} %copy.9.bias_ref, bf16[128,1152]{1,0:T(8,128)(2,1)S(1)} %collective-permute-done.refs_0_, bf16[128,1152]{1,0:T(8,128)(2,1)S(1)} %collective-permute-done.5.refs_1_, ...), custom_call_target="tpu_custom_call" | custom-call | flops 18119393280 | bytes 4128768 | tf_op jit(solution)/shard_map/pallas_call | solution.py:95
  95.1 0.8 shard_map.70.refs_6_
  96.0 2.5 %shard_map.71 = (f32[128,1152]{1,0:T(8,128)}, f32[128,1152]{1,0:T(8,128)}) custom-call(f32[1]{0:T(128)S(6)} %copy.8.scale_ref, f32[1]{0:T(128)S(6)} %copy.9.bias_ref, bf16[128,1152]{1,0:T(8,128)(2,1)S(1)} %collective-permute-done.1.refs_0_, bf16[128,1152]{1,0:T(8,128)(2,1)S(1)} %collective-permute-done.3.refs_1_, ...), custom_call_target="tpu_custom_call" | custom-call | flops 12079595520 | bytes 3538944 | tf_op jit(solution)/shard_map/pallas_call | solution.py:95
  (10 shorter events, 0.1 us)
Async XLA Ops:
  0.6 64.7 %copy-start.2 = (s32[128]{0:T(128)S(1)}, s32[128]{0:T(128)}, u32[]{:S(2)}) copy-start(s32[128]{0:T(128)} %param.7) | copy-start | bytes 1540
  0.6 44.4 %collective-permute-start = (bf16[128,1152]{1,0:T(8,128)(2,1)}, bf16[128,1152]{1,0:T(8,128)(2,1)S(1)}, u32[]{:S(2)}, u32[]{:S(2)}) collective-permute-start(bf16[128,1152]{1,0:T(8,128)(2,1)} %refs_5_.1), channel_id=1, source_target_pairs={{0,2},{1,3},{2,0},{3,1},{4,6},{5,7},{6,4},{7,5},{8,10},{9,11},{10,... | collective-permute-start | bytes 884744 | tf_op jit(solution)/shard_map/ppermute | solution.py:29
  20.6 26.4 %collective-permute-start.2 = (bf16[128,1152]{1,0:T(8,128)(2,1)}, bf16[128,1152]{1,0:T(8,128)(2,1)S(1)}, u32[]{:S(2)}, u32[]{:S(2)}) collective-permute-start(bf16[128,1152]{1,0:T(8,128)(2,1)} %refs_3_.1), channel_id=1, source_target_pairs={{0,2},{1,3},{2,0},{3,1},{4,6},{5,7},{6,4},{7,5},{8,10},{9,11},{10,... | collective-permute-start | bytes 884744 | tf_op jit(solution)/shard_map/ppermute | solution.py:29
  22.5 60.3 %collective-permute-start.5 = (bf16[128,1152]{1,0:T(8,128)(2,1)}, bf16[128,1152]{1,0:T(8,128)(2,1)S(1)}, u32[]{:S(2)}, u32[]{:S(2)}) collective-permute-start(bf16[128,1152]{1,0:T(8,128)(2,1)} %refs_5_.1), channel_id=1, source_target_pairs={{0,4},{1,5},{2,6},{3,7},{4,8},{5,9},{6,10},{7,11},{8,12},{9,13},{1... | collective-permute-start | bytes 884744 | tf_op jit(solution)/shard_map/ppermute | solution.py:23
  25.6 57.2 %collective-permute-start.6 = (bf16[128,1152]{1,0:T(8,128)(2,1)}, bf16[128,1152]{1,0:T(8,128)(2,1)S(1)}, u32[]{:S(2)}, u32[]{:S(2)}) collective-permute-start(bf16[128,1152]{1,0:T(8,128)(2,1)} %refs_3_.1), channel_id=1, source_target_pairs={{0,1022},{1,1023},{2,1020},{3,1021},{4,0},{5,1},{6,2},{7,3},{8,4},... | collective-permute-start | bytes 884744 | tf_op jit(solution)/shard_map/ppermute | solution.py:23
  41.6 50.5 %collective-permute-start.8 = (bf16[256,1152]{1,0:T(8,128)(2,1)S(1)}, bf16[256,1152]{1,0:T(8,128)(2,1)S(1)}, u32[]{:S(2)}, u32[]{:S(2)}) collective-permute-start(bf16[256,1152]{1,0:T(8,128)(2,1)S(1)} %pad_maximum_fusion.2), channel_id=1, source_target_pairs={{0,1},{1,0},{2,3},{3,2},{4,5},{5,4},{6,7},{7,6},{8,9},{9,8},{10,11... | collective-permute-start | bytes 1769480 | tf_op jit(solution)/shard_map/ppermute | solution.py:29
  45.0 44.5 %collective-permute-start.1 = (bf16[128,1152]{1,0:T(8,128)(2,1)S(1)}, bf16[128,1152]{1,0:T(8,128)(2,1)S(1)}, u32[]{:S(2)}, u32[]{:S(2)}) collective-permute-start(bf16[128,1152]{1,0:T(8,128)(2,1)S(1)} %collective-permute-done.refs_0_), channel_id=1, source_target_pairs={{0,4},{1,5},{2,6},{3,7},{4,8},{5,9},{6,10},{7,11},{8,12},{9,13},{1... | collective-permute-start | bytes 884744 | tf_op jit(solution)/shard_map/ppermute | solution.py:23
  47.0 42.6 %collective-permute-start.3 = (bf16[128,1152]{1,0:T(8,128)(2,1)S(1)}, bf16[128,1152]{1,0:T(8,128)(2,1)S(1)}, u32[]{:S(2)}, u32[]{:S(2)}) collective-permute-start(bf16[128,1152]{1,0:T(8,128)(2,1)S(1)} %collective-permute-done.2.refs_0_), channel_id=1, source_target_pairs={{0,1022},{1,1023},{2,1020},{3,1021},{4,0},{5,1},{6,2},{7,3},{8,4},... | collective-permute-start | bytes 884744 | tf_op jit(solution)/shard_map/ppermute | solution.py:23
  82.9 9.2 %copy-start = (bf16[128,1152]{1,0:T(8,128)(2,1)S(1)}, bf16[128,1152]{1,0:T(8,128)(2,1)}, u32[]{:S(2)}) copy-start(bf16[128,1152]{1,0:T(8,128)(2,1)} %refs_5_.1) | copy-start | bytes 884740
  82.9 9.2 %copy-start.1 = (bf16[128,1152]{1,0:T(8,128)(2,1)S(1)}, bf16[128,1152]{1,0:T(8,128)(2,1)}, u32[]{:S(2)}) copy-start(bf16[128,1152]{1,0:T(8,128)(2,1)} %refs_3_.1) | copy-start | bytes 884740
  82.9 10.5 %collective-permute-start.7 = (bf16[384,1152]{1,0:T(8,128)(2,1)S(1)}, bf16[384,1152]{1,0:T(8,128)(2,1)S(1)}, u32[]{:S(2)}, u32[]{:S(2)}) collective-permute-start(bf16[384,1152]{1,0:T(8,128)(2,1)S(1)} %pad_maximum_fusion), channel_id=1, source_target_pairs={{0,1},{1,0},{2,3},{3,2},{4,5},{5,4},{6,7},{7,6},{8,9},{9,8},{10,11... | collective-permute-start | bytes 2654216 | tf_op jit(solution)/shard_map/ppermute | solution.py:29
  87.6 7.5 %collective-permute-start.9 = (bf16[128,1152]{1,0:T(8,128)(2,1)S(1)}, bf16[128,1152]{1,0:T(8,128)(2,1)S(1)}, u32[]{:S(2)}, u32[]{:S(2)}) collective-permute-start(bf16[128,1152]{1,0:T(8,128)(2,1)S(1)} %collective-permute-done.2.refs_0_), channel_id=1, source_target_pairs={{0,1},{1,0},{2,3},{3,2},{4,5},{5,4},{6,7},{7,6},{8,9},{9,8},{10,11... | collective-permute-start | bytes 884744 | tf_op jit(solution)/shard_map/ppermute | solution.py:29
  89.6 6.3 %collective-permute-start.4 = (bf16[256,1152]{1,0:T(8,128)(2,1)S(1)}, bf16[256,1152]{1,0:T(8,128)(2,1)S(1)}, u32[]{:S(2)}, u32[]{:S(2)}) collective-permute-start(bf16[256,1152]{1,0:T(8,128)(2,1)S(1)} %pad_maximum_fusion.1), channel_id=1, source_target_pairs={{0,1},{1,0},{2,3},{3,2},{4,5},{5,4},{6,7},{7,6},{8,9},{9,8},{10,11... | collective-permute-start | bytes 1769480 | tf_op jit(solution)/shard_map/ppermute | solution.py:29

commit v5 on v4

--- a/solution.py
+++ b/solution.py
@@ -10,7 +10,7 @@
 norm_eps = 1e-06
 RUN = 32
 ROWS = 128
-WEIGHTS = (40, 40, 40, 40)
+WEIGHTS = (120, 120, 120, 120)
 
 
 def moved_block(value, steps):
@@ -124,27 +124,24 @@
     last_text = moved_block(text, 1)
     next_image = moved_block(image, -1)
     twin = moved_core(jnp.concatenate([text, image]))
+    far_last_text = moved_block(far_text, 1)
+    far_next_image = moved_block(far_image, -1)
+    far_twin = moved_core(jnp.concatenate([far_text, far_image]))
+    last_twin = moved_core(jnp.concatenate([last_text, far_last_text, next_image, far_next_image]))
     sums = first_terms(scalars, image, text, positives, [twin], [(0, 0)], [(0, ROWS)])
-    far_last_text = moved_block(far_text, 1)
-    mid_twin = moved_core(jnp.concatenate([far_text, last_text, next_image]))
-    sums = next_terms(
+    image_sum, text_sum = next_terms(
         1,
         scalars,
-        [far_text, last_text, next_image, mid_twin],
-        (image, sums[0], [(0, 0), (1, 0), (3, 0), (3, ROWS)], False),
-        (text, sums[1], [(2, 0), (3, 2 * ROWS)], False),
+        [far_text, far_image, far_twin, last_text, far_last_text, next_image, far_next_image],
+        (image, sums[0], [(0, 0), (2, 0), (3, 0), (4, 0)], False),
+        (text, sums[1], [(1, 0), (2, ROWS), (5, 0), (6, 0)], False),
     )
-    far_next_image = moved_block(far_image, -1)
-    image_sum, text_sum = sums
-    image_twin = moved_core(far_image)
-    (text_sum,) = next_terms(2, scalars, [far_image, image_twin], (text, text_sum, [(0, 0), (1, 0)], False))
-    last_twin = moved_core(jnp.concatenate([far_last_text, far_next_image]))
     return next_terms(
         3,
         scalars,
-        [far_last_text, far_next_image, last_twin],
-        (image, image_sum, [(0, 0), (2, 0)], True),
-        (text, text_sum, [(1, 0), (2, ROWS)], True),
+        [last_twin],
+        (image, image_sum, [(0, 0), (0, ROWS)], True),
+        (text, text_sum, [(0, 2 * ROWS), (0, 3 * ROWS)], True),
     )
 
 

time: 98.9 us -> 97.9 us (0.990)
  starting transfers between devices: 71.2 us -> 60.8 us
  waiting for transfers between devices: 17.4 us -> 26.7 us
    ppermute x4, starting transfers between devices: 36.9 us -> 23 us  [moved_block(): return lax.ppermute(value, AXES, pairs)]
    ppermute x4, waiting for transfers between devices: 17.4 us -> 26.7 us  [moved_block(): return lax.ppermute(value, AXES, pairs)]
    ppermute x6 -> x5, starting transfers between devices: 34.3 us -> 37.8 us  [moved_group(): return lax.ppermute(value, AXES, pairs)]
    pallas_call x4 -> x3, Pallas kernels: 6.37 us -> 5.75 us  [call(): pl.pallas_call(body, out_shape=(out,) * outs, in_specs=[SMEM] * 2 + [VMEM...]
  transfers between devices with their start and end apart: 10 -> 9, of which waited for: 1 -> 4; matrix products, arithmetic and copies ran while one was open for 1% -> 2% of each run, Pallas kernels for 4% -> 3%
where the time goes in v5:
time: 97.9 us; the launch traced here: 97.5 us
  starting transfers between devices  60.8 us (62%)
  waiting for transfers between devices  26.7 us (27%)
  Pallas kernels  5.75 us (6%)
  between operations  2.1 us (2%)
  other arithmetic  2.05 us (2%)
    ppermute x5, starting transfers between devices, moved_group(): return lax.ppermute(value, AXES, pairs)  37.8 us
    ppermute x4, waiting for transfers between devices, moved_block(): return lax.ppermute(value, AXES, pairs)  26.7 us
    ppermute x4, starting transfers between devices, moved_block(): return lax.ppermute(value, AXES, pairs)  23 us
    pallas_call x3, Pallas kernels, call(): pl.pallas_call(body, out_shape=(out,) * outs, in_specs=[SMEM] * 2 + [VMEM...  5.75 us
  transfers between devices with their start and end apart: 9, of which 4 were waited for; matrix products, arithmetic and copies ran while one was open for 2% of the time, Pallas kernels for 3%

profile of v5, /device:TPU:1, one launch (start us, length us, event | category | flops | bytes accessed | tf_op | source)
XLA Modules:
  0.0 97.5 jit_solution(11645173925827409696)
XLA Ops:
  0.7 20.0 %collective-permute-start.4 = (bf16[128,1152]{1,0:T(8,128)(2,1)}, bf16[128,1152]{1,0:T(8,128)(2,1)S(1)}, u32[]{:S(2)}, u32[]{:S(2)}) collective-permute-start(bf16[128,1152]{1,0:T(8,128)(2,1)} %refs_1_.1), channel_id=1, source_target_pairs={{0,2},{1,3},{2,0},{3,1},{4,6},{5,7},{6,4},{7,5},{8,10},{9,11},{10,... | collective-permute-start | bytes 884744 | tf_op jit(solution)/shard_map/ppermute | solution.py:29
  20.7 1.9 %collective-permute-start.1 = (bf16[128,1152]{1,0:T(8,128)(2,1)}, bf16[128,1152]{1,0:T(8,128)(2,1)S(1)}, u32[]{:S(2)}, u32[]{:S(2)}) collective-permute-start(bf16[128,1152]{1,0:T(8,128)(2,1)} %refs_3_.1), channel_id=1, source_target_pairs={{0,2},{1,3},{2,0},{3,1},{4,6},{5,7},{6,4},{7,5},{8,10},{9,11},{10,... | collective-permute-start | bytes 884744 | tf_op jit(solution)/shard_map/ppermute | solution.py:29
  22.6 1.9 %pad_maximum_fusion.2 = bf16[256,1152]{1,0:T(8,128)(2,1)} fusion(bf16[128,1152]{1,0:T(8,128)(2,1)} %refs_1_.1, bf16[128,1152]{1,0:T(8,128)(2,1)} %refs_3_.1), kind=kLoop, calls=%fused_computation.2 | loop fusion | flops 1179648 | bytes 1179648 | tf_op jit(solution)/shard_map/concatenate | solution.py:126
  24.5 8.8 %collective-permute-start.8 = (bf16[256,1152]{1,0:T(8,128)(2,1)}, bf16[256,1152]{1,0:T(8,128)(2,1)S(1)}, u32[]{:S(2)}, u32[]{:S(2)}) collective-permute-start(bf16[256,1152]{1,0:T(8,128)(2,1)} %pad_maximum_fusion.2), channel_id=1, source_target_pairs={{0,1},{1,0},{2,3},{3,2},{4,5},{5,4},{6,7},{7,6},{8,9},{9,8},{10,11... | collective-permute-start | bytes 1769480 | tf_op jit(solution)/shard_map/ppermute | solution.py:29
  33.3 10.4 %collective-permute-start.3 = (bf16[128,1152]{1,0:T(8,128)(2,1)S(1)}, bf16[128,1152]{1,0:T(8,128)(2,1)S(1)}, u32[]{:S(2)}, u32[]{:S(2)}) collective-permute-start(bf16[128,1152]{1,0:T(8,128)(2,1)S(1)} %copy-done), channel_id=1, source_target_pairs={{0,1022},{1,1023},{2,1020},{3,1021},{4,0},{5,1},{6,2},{7,3},{8,4},... | collective-permute-start | bytes 884744 | tf_op jit(solution)/shard_map/ppermute | solution.py:23
  43.8 1.9 %collective-permute-start = (bf16[128,1152]{1,0:T(8,128)(2,1)S(1)}, bf16[128,1152]{1,0:T(8,128)(2,1)S(1)}, u32[]{:S(2)}, u32[]{:S(2)}) collective-permute-start(bf16[128,1152]{1,0:T(8,128)(2,1)S(1)} %copy-done.1), channel_id=1, source_target_pairs={{0,4},{1,5},{2,6},{3,7},{4,8},{5,9},{6,10},{7,11},{8,12},{9,13},{1... | collective-permute-start | bytes 884744 | tf_op jit(solution)/shard_map/ppermute | solution.py:23
  45.7 0.0 collective-permute-done.4.refs_1_
  45.7 8.8 %collective-permute-start.5 = (bf16[128,1152]{1,0:T(8,128)(2,1)S(1)}, bf16[128,1152]{1,0:T(8,128)(2,1)S(1)}, u32[]{:S(2)}, u32[]{:S(2)}) collective-permute-start(bf16[128,1152]{1,0:T(8,128)(2,1)S(1)} %collective-permute-done.4.refs_1_), channel_id=1, source_target_pairs={{0,1022},{1,1023},{2,1020},{3,1021},{4,0},{5,1},{6,2},{7,3},{8,4},... | collective-permute-start | bytes 884744 | tf_op jit(solution)/shard_map/ppermute | solution.py:23
  54.5 0.0 collective-permute-done.1.refs_0_
  54.5 1.9 %collective-permute-start.2 = (bf16[128,1152]{1,0:T(8,128)(2,1)S(1)}, bf16[128,1152]{1,0:T(8,128)(2,1)S(1)}, u32[]{:S(2)}, u32[]{:S(2)}) collective-permute-start(bf16[128,1152]{1,0:T(8,128)(2,1)S(1)} %collective-permute-done.1.refs_0_), channel_id=1, source_target_pairs={{0,4},{1,5},{2,6},{3,7},{4,8},{5,9},{6,10},{7,11},{8,12},{9,13},{1... | collective-permute-start | bytes 884744 | tf_op jit(solution)/shard_map/ppermute | solution.py:23
  57.7 0.1 copy.7.pos_ref
  57.9 21.3 %collective-permute-done.3.refs_5_ = bf16[128,1152]{1,0:T(8,128)(2,1)S(1)} collective-permute-done((bf16[128,1152]{1,0:T(8,128)(2,1)S(1)}, bf16[128,1152]{1,0:T(8,128)(2,1)S(1)}, u32[]{:S(2)}, u32[]{:S(2)}) %collective-permute-start.3) | collective-permute-done | bytes 294944 | tf_op jit(solution)/shard_map/ppermute | solution.py:23
  79.2 2.4 %collective-permute-start.7 = (bf16[256,1152]{1,0:T(8,128)(2,1)S(1)}, bf16[256,1152]{1,0:T(8,128)(2,1)S(1)}, u32[]{:S(2)}, u32[]{:S(2)}) collective-permute-start(bf16[256,1152]{1,0:T(8,128)(2,1)S(1)} %pad_maximum_fusion.1), channel_id=1, source_target_pairs={{0,1},{1,0},{2,3},{3,2},{4,5},{5,4},{6,7},{7,6},{8,9},{9,8},{10,11... | collective-permute-start | bytes 1769480 | tf_op jit(solution)/shard_map/ppermute | solution.py:29
  81.6 1.3 %collective-permute-done.refs_3_ = bf16[128,1152]{1,0:T(8,128)(2,1)S(1)} collective-permute-done((bf16[128,1152]{1,0:T(8,128)(2,1)S(1)}, bf16[128,1152]{1,0:T(8,128)(2,1)S(1)}, u32[]{:S(2)}, u32[]{:S(2)}) %collective-permute-start) | collective-permute-done | bytes 294944 | tf_op jit(solution)/shard_map/ppermute | solution.py:23
  82.9 2.6 %collective-permute-done.5.refs_6_ = bf16[128,1152]{1,0:T(8,128)(2,1)S(1)} collective-permute-done((bf16[128,1152]{1,0:T(8,128)(2,1)S(1)}, bf16[128,1152]{1,0:T(8,128)(2,1)S(1)}, u32[]{:S(2)}, u32[]{:S(2)}) %collective-permute-start.5) | collective-permute-done | bytes 294944 | tf_op jit(solution)/shard_map/ppermute | solution.py:23
  85.5 1.4 %collective-permute-done.2.refs_4_ = bf16[128,1152]{1,0:T(8,128)(2,1)S(1)} collective-permute-done((bf16[128,1152]{1,0:T(8,128)(2,1)S(1)}, bf16[128,1152]{1,0:T(8,128)(2,1)S(1)}, u32[]{:S(2)}, u32[]{:S(2)}) %collective-permute-start.2) | collective-permute-done | bytes 294944 | tf_op jit(solution)/shard_map/ppermute | solution.py:23
  86.9 0.1 pad_maximum_fusion
  87.0 4.7 %collective-permute-start.6 = (bf16[512,1152]{1,0:T(8,128)(2,1)S(1)}, bf16[512,1152]{1,0:T(8,128)(2,1)S(1)}, u32[]{:S(2)}, u32[]{:S(2)}) collective-permute-start(bf16[512,1152]{1,0:T(8,128)(2,1)S(1)} %pad_maximum_fusion), channel_id=1, source_target_pairs={{0,1},{1,0},{2,3},{3,2},{4,5},{5,4},{6,7},{7,6},{8,9},{9,8},{10,11... | collective-permute-start | bytes 3538952 | tf_op jit(solution)/shard_map/ppermute | solution.py:29
  91.7 0.0 collective-permute-done.8.refs_0_
  91.7 1.3 %shard_map.68 = (f32[128,1152]{1,0:T(8,128)S(1)}, f32[128,1152]{1,0:T(8,128)S(1)}) custom-call(f32[1]{0:T(128)S(6)} %copy.8.scale_ref, f32[1]{0:T(128)S(6)} %copy.9.bias_ref, bf16[128,1152]{1,0:T(8,128)(2,1)S(1)} %copy-done, bf16[128,1152]{1,0:T(8,128)(2,1)S(1)} %copy-done.1, s32[128,1]{1,0:T(8,128)S(1)} %copy.7.pos_ref, ...), custom_call_target="tpu_custom_call" | custom-call | flops 36238786560 | bytes 3538944 | tf_op jit(solution)/shard_map/pallas_call | solution.py:95
  93.0 0.0 collective-permute-done.7.refs_2_
  93.0 1.9 %shard_map.69 = (f32[128,1152]{1,0:T(8,128)S(1)}, f32[128,1152]{1,0:T(8,128)S(1)}) custom-call(f32[1]{0:T(128)S(6)} %copy.8.scale_ref, f32[1]{0:T(128)S(6)} %copy.9.bias_ref, bf16[128,1152]{1,0:T(8,128)(2,1)S(1)} %collective-permute-done.1.refs_0_, bf16[128,1152]{1,0:T(8,128)(2,1)S(1)} %collective-permute-done.4.refs_1_, ...), custom_call_target="tpu_custom_call" | custom-call | flops 72477573120 | bytes 4718592 | tf_op jit(solution)/shard_map/pallas_call | solution.py:95
  95.0 0.0 collective-permute-done.6.refs_0_
  95.0 2.5 %shard_map.70 = (f32[128,1152]{1,0:T(8,128)}, f32[128,1152]{1,0:T(8,128)}) custom-call(f32[1]{0:T(128)S(6)} %copy.8.scale_ref, f32[1]{0:T(128)S(6)} %copy.9.bias_ref, bf16[512,1152]{1,0:T(8,128)(2,1)S(1)} %collective-permute-done.6.refs_0_, bf16[128,1152]{1,0:T(8,128)(2,1)S(1)} %copy-done, f32[128,1152]{1,0:T(8,128)S(1)} %get-tuple-element.8.refs_2_, ...), custom_call_target="tpu_custom_call" | custom-call | flops 36238786560 | bytes 3538944 | tf_op jit(solution)/shard_map/pallas_call | solution.py:95
  (7 shorter events, 0.1 us)
Async XLA Ops:
  0.6 32.7 %copy-start = (bf16[128,1152]{1,0:T(8,128)(2,1)S(1)}, bf16[128,1152]{1,0:T(8,128)(2,1)}, u32[]{:S(2)}) copy-start(bf16[128,1152]{1,0:T(8,128)(2,1)} %refs_1_.1) | copy-start | bytes 884740
  0.6 43.1 %copy-start.1 = (bf16[128,1152]{1,0:T(8,128)(2,1)S(1)}, bf16[128,1152]{1,0:T(8,128)(2,1)}, u32[]{:S(2)}) copy-start(bf16[128,1152]{1,0:T(8,128)(2,1)} %refs_3_.1) | copy-start | bytes 884740
  0.6 57.1 %copy-start.2 = (s32[128]{0:T(128)S(1)}, s32[128]{0:T(128)}, u32[]{:S(2)}) copy-start(s32[128]{0:T(128)} %param.7) | copy-start | bytes 1540
  0.7 45.0 %collective-permute-start.4 = (bf16[128,1152]{1,0:T(8,128)(2,1)}, bf16[128,1152]{1,0:T(8,128)(2,1)S(1)}, u32[]{:S(2)}, u32[]{:S(2)}) collective-permute-start(bf16[128,1152]{1,0:T(8,128)(2,1)} %refs_1_.1), channel_id=1, source_target_pairs={{0,2},{1,3},{2,0},{3,1},{4,6},{5,7},{6,4},{7,5},{8,10},{9,11},{10,... | collective-permute-start | bytes 884744 | tf_op jit(solution)/shard_map/ppermute | solution.py:29
  20.7 33.8 %collective-permute-start.1 = (bf16[128,1152]{1,0:T(8,128)(2,1)}, bf16[128,1152]{1,0:T(8,128)(2,1)S(1)}, u32[]{:S(2)}, u32[]{:S(2)}) collective-permute-start(bf16[128,1152]{1,0:T(8,128)(2,1)} %refs_3_.1), channel_id=1, source_target_pairs={{0,2},{1,3},{2,0},{3,1},{4,6},{5,7},{6,4},{7,5},{8,10},{9,11},{10,... | collective-permute-start | bytes 884744 | tf_op jit(solution)/shard_map/ppermute | solution.py:29
  24.5 67.2 %collective-permute-start.8 = (bf16[256,1152]{1,0:T(8,128)(2,1)}, bf16[256,1152]{1,0:T(8,128)(2,1)S(1)}, u32[]{:S(2)}, u32[]{:S(2)}) collective-permute-start(bf16[256,1152]{1,0:T(8,128)(2,1)} %pad_maximum_fusion.2), channel_id=1, source_target_pairs={{0,1},{1,0},{2,3},{3,2},{4,5},{5,4},{6,7},{7,6},{8,9},{9,8},{10,11... | collective-permute-start | bytes 1769480 | tf_op jit(solution)/shard_map/ppermute | solution.py:29
  33.3 45.9 %collective-permute-start.3 = (bf16[128,1152]{1,0:T(8,128)(2,1)S(1)}, bf16[128,1152]{1,0:T(8,128)(2,1)S(1)}, u32[]{:S(2)}, u32[]{:S(2)}) collective-permute-start(bf16[128,1152]{1,0:T(8,128)(2,1)S(1)} %copy-done), channel_id=1, source_target_pairs={{0,1022},{1,1023},{2,1020},{3,1021},{4,0},{5,1},{6,2},{7,3},{8,4},... | collective-permute-start | bytes 884744 | tf_op jit(solution)/shard_map/ppermute | solution.py:23
  43.8 39.2 %collective-permute-start = (bf16[128,1152]{1,0:T(8,128)(2,1)S(1)}, bf16[128,1152]{1,0:T(8,128)(2,1)S(1)}, u32[]{:S(2)}, u32[]{:S(2)}) collective-permute-start(bf16[128,1152]{1,0:T(8,128)(2,1)S(1)} %copy-done.1), channel_id=1, source_target_pairs={{0,4},{1,5},{2,6},{3,7},{4,8},{5,9},{6,10},{7,11},{8,12},{9,13},{1... | collective-permute-start | bytes 884744 | tf_op jit(solution)/shard_map/ppermute | solution.py:23
  45.7 39.9 %collective-permute-start.5 = (bf16[128,1152]{1,0:T(8,128)(2,1)S(1)}, bf16[128,1152]{1,0:T(8,128)(2,1)S(1)}, u32[]{:S(2)}, u32[]{:S(2)}) collective-permute-start(bf16[128,1152]{1,0:T(8,128)(2,1)S(1)} %collective-permute-done.4.refs_1_), channel_id=1, source_target_pairs={{0,1022},{1,1023},{2,1020},{3,1021},{4,0},{5,1},{6,2},{7,3},{8,4},... | collective-permute-start | bytes 884744 | tf_op jit(solution)/shard_map/ppermute | solution.py:23
  54.5 32.4 %collective-permute-start.2 = (bf16[128,1152]{1,0:T(8,128)(2,1)S(1)}, bf16[128,1152]{1,0:T(8,128)(2,1)S(1)}, u32[]{:S(2)}, u32[]{:S(2)}) collective-permute-start(bf16[128,1152]{1,0:T(8,128)(2,1)S(1)} %collective-permute-done.1.refs_0_), channel_id=1, source_target_pairs={{0,4},{1,5},{2,6},{3,7},{4,8},{5,9},{6,10},{7,11},{8,12},{9,13},{1... | collective-permute-start | bytes 884744 | tf_op jit(solution)/shard_map/ppermute | solution.py:23
  79.2 13.8 %collective-permute-start.7 = (bf16[256,1152]{1,0:T(8,128)(2,1)S(1)}, bf16[256,1152]{1,0:T(8,128)(2,1)S(1)}, u32[]{:S(2)}, u32[]{:S(2)}) collective-permute-start(bf16[256,1152]{1,0:T(8,128)(2,1)S(1)} %pad_maximum_fusion.1), channel_id=1, source_target_pairs={{0,1},{1,0},{2,3},{3,2},{4,5},{5,4},{6,7},{7,6},{8,9},{9,8},{10,11... | collective-permute-start | bytes 1769480 | tf_op jit(solution)/shard_map/ppermute | solution.py:29
  87.0 7.9 %collective-permute-start.6 = (bf16[512,1152]{1,0:T(8,128)(2,1)S(1)}, bf16[512,1152]{1,0:T(8,128)(2,1)S(1)}, u32[]{:S(2)}, u32[]{:S(2)}) collective-permute-start(bf16[512,1152]{1,0:T(8,128)(2,1)S(1)} %pad_maximum_fusion), channel_id=1, source_target_pairs={{0,1},{1,0},{2,3},{3,2},{4,5},{5,4},{6,7},{7,6},{8,9},{9,8},{10,11... | collective-permute-start | bytes 3538952 | tf_op jit(solution)/shard_map/ppermute | solution.py:29
